TPU v7x, 512 devices: a whole 4x8x8 slice. The times are simulated.
512 devices in a mesh: pair: 4 (over x), src: 8 (over z), tgt: 16 (over y, core).
Axes of the slice: x: 4, y: 8, z: 8, core: 2. Of those that a mesh axis runs over, the one named last changes fastest.
Arguments:
- src_cells: float32 [4, 30, 4096], P('pair', None, 'src'), may hold values from -17 to 17
- final_cells: float32 [30, 4096], P(None, 'tgt'), may hold values from -17 to 17
- growth: float32 [4, 4096], P('pair', 'src'), may hold values from 0.5 to 2
- live: int32 [5], replicated, may hold values from 1024 to 4096, as said below
- final_fates: float32 [40, 4096], P(None, 'tgt'), may hold values from 0 to 1
Outputs:
- fate_maps: float32 [4, 40, 4096], P('pair', None, ('src', 'tgt'))
- potentials: float32 [4, 4096], P('pair', 'src')
Inputs may be any that keep to these rules, and one draw needn't show every extreme that they name: `live`: every count is at least 1024 and one snapshot fills all 4096 slots.
All inputs are finite; a program needn't handle non-finite values.
Results may differ from a plain program's by a relative error of at most 0.0049.
Values may be sent and summed in bfloat16 or wider, within the bound.
A program may use at most 64 MiB of HBM per device.

v0:
```python
import jax
import jax.numpy as jnp
from jax import lax
from jax.sharding import PartitionSpec as P

ITERS = 8


EPS = 0.1
LAM = 1.0
NEG = -1e30


def joined(shard, axis, combine):
    everything = jax.tree.map(lambda part: lax.all_gather(part, axis), shard)
    leading = jax.tree.map(lambda part: part[0], everything)

    def step(k, so_far):
        return combine(so_far, jax.tree.map(lambda part: part[k], everything))

    return lax.fori_loop(1, lax.axis_size(axis), step, leading)


def shifted(shard, axis, by):
    devices = lax.axis_size(axis)
    pairs = [(i, i + by) for i in range(devices) if 0 <= i + by < devices]
    return lax.ppermute(shard, axis, pairs)


def from_root(shard, axis, root):
    mine = lax.axis_index(axis) == root
    return lax.psum(jnp.where(mine, shard, jnp.zeros_like(shard)), axis)


def combine(first, second):
    peak = jnp.maximum(first[0], second[0])
    return (peak, first[1] * jnp.exp(first[0] - peak) + second[1] * jnp.exp(second[0] - peak))


def column_lse(col_scores):
    peak = jnp.max(col_scores, axis=0)
    totals = jnp.sum(jnp.exp(col_scores - peak[None, :]), axis=0)
    return joined((peak, totals), "src", combine)


def row_lse(row_scores):
    peak = jnp.max(row_scores, axis=1)
    totals = jnp.sum(jnp.exp(row_scores - peak[:, None]), axis=1)
    return joined((peak, totals), "tgt", combine)


def local(src_cells, final_cells, growth, live, final_fates):
    pair_count = lax.axis_size("pair")
    src_count = lax.axis_size("src")
    tgt_count = lax.axis_size("tgt")
    pair_rank = lax.axis_index("pair")
    src_rank = lax.axis_index("src")
    tgt_rank = lax.axis_index("tgt")
    shrink = LAM / (LAM + EPS)
    source_pos = src_cells[0]
    src_width = source_pos.shape[1]
    tgt_width = final_cells.shape[1]
    share_width = src_width // tgt_count
    tgt_ratio = tgt_count // src_count
    owner_rank = tgt_rank // tgt_ratio
    offset_in = tgt_rank % tgt_ratio * tgt_width
    is_last = pair_rank == pair_count - 1
    arrived = shifted(source_pos, "pair", -1)
    owner_cells = from_root(arrived, "src", owner_rank)
    target_pos = jnp.where(
        is_last, final_cells, lax.dynamic_slice_in_dim(owner_cells, offset_in, tgt_width, 1)
    )
    cross = lax.dot_general(
        source_pos,
        target_pos,
        (((0,), (0,)), ((), ())),
        precision=lax.Precision.HIGHEST,
        preferred_element_type=jnp.float32,
    )
    src_sq = jnp.sum(source_pos * source_pos, axis=0)
    tgt_sq = jnp.sum(target_pos * target_pos, axis=0)
    cost_tile = (src_sq[:, None] + tgt_sq[None, :] - 2.0 * cross) / (2.0 * source_pos.shape[0])
    live_now = lax.dynamic_index_in_dim(live, pair_rank, keepdims=False)
    live_next = lax.dynamic_index_in_dim(live, pair_rank + 1, keepdims=False)
    src_index = src_rank * src_width + jnp.arange(src_width, dtype=jnp.int32)
    tgt_index = tgt_rank * tgt_width + jnp.arange(tgt_width, dtype=jnp.int32)
    share_index = (src_rank * tgt_count + tgt_rank) * share_width + jnp.arange(
        share_width, dtype=jnp.int32
    )
    live_src = src_index < live_now
    live_tgt = tgt_index < live_next
    live_share = share_index < live_now
    log_mass_a = jnp.where(
        live_src, jnp.log(growth[0]) - jnp.log(live_now.astype(jnp.float32)), NEG
    )
    log_mass_b = jnp.where(
        live_tgt, -jnp.log(live_next.astype(jnp.float32)) * jnp.ones((tgt_width,), jnp.float32), NEG
    )
    pot_src = jnp.zeros((src_width,), jnp.float32)
    pot_tgt = jnp.zeros((tgt_width,), jnp.float32)
    for step_num in range(ITERS):
        col_scores = (pot_src[:, None] - cost_tile) / EPS + log_mass_a[:, None]
        col_peak, col_total = column_lse(col_scores)
        pot_tgt = -shrink * EPS * (col_peak + jnp.log(col_total))
        row_scores = (pot_tgt[None, :] - cost_tile) / EPS + log_mass_b[None, :]
        row_peak, row_total = row_lse(row_scores)
        pot_src = -shrink * EPS * (row_peak + jnp.log(row_total))
    weights = (jnp.exp(row_scores - row_peak[:, None]) / row_total[:, None]).astype(jnp.bfloat16)
    handed = jnp.where(
        is_last, final_fates.astype(jnp.bfloat16), jnp.zeros(final_fates.shape, jnp.bfloat16)
    )
    fate_maps = jnp.zeros((final_fates.shape[0], share_width), jnp.float32)
    for section_num in range(pair_count):
        active = pair_count - 1 - section_num
        partial_value = lax.dot_general(
            handed, weights, (((1,), (1,)), ((), ())), preferred_element_type=jnp.float32
        )
        fate_share = lax.psum_scatter(partial_value, "tgt", scatter_dimension=1, tiled=True)
        fate_share = jnp.where(live_share[None, :], fate_share, 0.0)
        fate_maps = jnp.where(pair_rank == active, fate_share, fate_maps)
        if section_num + 1 < pair_count:
            passed = shifted(fate_share.astype(jnp.bfloat16), "pair", -1)
            gathered = lax.all_gather(passed, ("src", "tgt"), axis=1, tiled=True)
            fresh = lax.dynamic_slice_in_dim(gathered, tgt_rank * tgt_width, tgt_width, 1)
            handed = jnp.where(pair_rank == active - 1, fresh, handed)
    return (fate_maps[None], pot_src[None])


def solution(mesh):
    placed = (P("pair", None, "src"), P(None, "tgt"), P("pair", "src"), P(), P(None, "tgt"))
    return jax.shard_map(
        local,
        mesh=mesh,
        in_specs=placed,
        out_specs=(P("pair", None, ("src", "tgt")), P("pair", "src")),
        check_vma=False,
    )
```

profile of v0, /device:TPU:1, one launch (start us, length us, event | category | flops | bytes accessed | tf_op | source)
XLA Modules:
  0.0 955.4 jit_solution(8507760095305894291)
XLA Ops:
  8.0 1.4 collective-permute-start
  14.4 30.1 %psum.7 = f32[30,512]{1,0:T(8,128)S(1)} all-reduce(f32[30,512]{1,0:T(8,128)S(1)} %broadcast_select_fusion), channel_id=1, replica_groups=mesh['pair'=4,'src'=8,'tgt'=16] {'src'}, use_global_device_ids=true, to_apply=%region_1.2 | all-reduce | flops 15360 | bytes 122880 | tf_op jit(solution)/shard_map/psum | solution.py:32
  45.6 9.9 %all-gather.33 = f32[8,1,256]{2,1,0:T(1,128)S(1)} all-gather(f32[1,1,256]{2,1,0:T(1,128)S(1)} %bitcast.410), channel_id=3, replica_groups=mesh['pair'=4,'src'=8,'tgt'=16] {'src'}, dimensions={0}, use_global_device_ids=true | all-gather | bytes 9216 | tf_op jit(solution)/shard_map/all_gather | solution.py:15
  56.1 11.2 %all-gather.32 = f32[8,1,256]{2,1,0:T(1,128)S(1)} all-gather(f32[1,1,256]{2,1,0:T(1,128)S(1)} %bitcast.402), channel_id=2, replica_groups=mesh['pair'=4,'src'=8,'tgt'=16] {'src'}, dimensions={0}, use_global_device_ids=true | all-gather | bytes 9216 | tf_op jit(solution)/shard_map/all_gather | solution.py:15
  69.3 32.7 %all-gather.35 = f32[16,1,512]{2,1,0:T(1,128)S(1)} all-gather(f32[1,1,512]{2,1,0:T(1,128)S(1)} %bitcast.393), channel_id=5, replica_groups=mesh['pair'=4,'src'=8,'tgt'=16] {'tgt'}, dimensions={0}, use_global_device_ids=true | all-gather | bytes 34816 | tf_op jit(solution)/shard_map/all_gather | solution.py:15
  102.7 15.0 %all-gather.34 = f32[16,1,512]{2,1,0:T(1,128)S(1)} all-gather(f32[1,1,512]{2,1,0:T(1,128)S(1)} %bitcast.378), channel_id=4, replica_groups=mesh['pair'=4,'src'=8,'tgt'=16] {'tgt'}, dimensions={0}, use_global_device_ids=true | all-gather | bytes 34816 | tf_op jit(solution)/shard_map/all_gather | solution.py:15
  120.2 9.8 %all-gather.36 = f32[8,1,256]{2,1,0:T(1,128)S(1)} all-gather(f32[1,1,256]{2,1,0:T(1,128)S(1)} %bitcast.387), channel_id=6, replica_groups=mesh['pair'=4,'src'=8,'tgt'=16] {'src'}, dimensions={0}, use_global_device_ids=true | all-gather | bytes 9216 | tf_op jit(solution)/shard_map/all_gather | solution.py:15
  130.6 11.4 %all-gather.37 = f32[8,1,256]{2,1,0:T(1,128)S(1)} all-gather(f32[1,1,256]{2,1,0:T(1,128)S(1)} %bitcast.404), channel_id=7, replica_groups=mesh['pair'=4,'src'=8,'tgt'=16] {'src'}, dimensions={0}, use_global_device_ids=true | all-gather | bytes 9216 | tf_op jit(solution)/shard_map/all_gather | solution.py:15
  144.0 22.8 %all-gather.39 = f32[16,1,512]{2,1,0:T(1,128)S(1)} all-gather(f32[1,1,512]{2,1,0:T(1,128)S(1)} %bitcast.394), channel_id=9, replica_groups=mesh['pair'=4,'src'=8,'tgt'=16] {'tgt'}, dimensions={0}, use_global_device_ids=true | all-gather | bytes 34816 | tf_op jit(solution)/shard_map/all_gather | solution.py:15
  167.4 15.0 %all-gather.38 = f32[16,1,512]{2,1,0:T(1,128)S(1)} all-gather(f32[1,1,512]{2,1,0:T(1,128)S(1)} %bitcast.379), channel_id=8, replica_groups=mesh['pair'=4,'src'=8,'tgt'=16] {'tgt'}, dimensions={0}, use_global_device_ids=true | all-gather | bytes 34816 | tf_op jit(solution)/shard_map/all_gather | solution.py:15
  184.9 9.8 %all-gather.40 = f32[8,1,256]{2,1,0:T(1,128)S(1)} all-gather(f32[1,1,256]{2,1,0:T(1,128)S(1)} %bitcast.388), channel_id=10, replica_groups=mesh['pair'=4,'src'=8,'tgt'=16] {'src'}, dimensions={0}, use_global_device_ids=true | all-gather | bytes 9216 | tf_op jit(solution)/shard_map/all_gather | solution.py:15
  194.8 11.4 %all-gather.41 = f32[8,1,256]{2,1,0:T(1,128)S(1)} all-gather(f32[1,1,256]{2,1,0:T(1,128)S(1)} %bitcast.405), channel_id=11, replica_groups=mesh['pair'=4,'src'=8,'tgt'=16] {'src'}, dimensions={0}, use_global_device_ids=true | all-gather | bytes 9216 | tf_op jit(solution)/shard_map/all_gather | solution.py:15
  206.9 22.8 %all-gather.43 = f32[16,1,512]{2,1,0:T(1,128)S(1)} all-gather(f32[1,1,512]{2,1,0:T(1,128)S(1)} %bitcast.395), channel_id=13, replica_groups=mesh['pair'=4,'src'=8,'tgt'=16] {'tgt'}, dimensions={0}, use_global_device_ids=true | all-gather | bytes 34816 | tf_op jit(solution)/shard_map/all_gather | solution.py:15
  230.3 15.0 %all-gather.42 = f32[16,1,512]{2,1,0:T(1,128)S(1)} all-gather(f32[1,1,512]{2,1,0:T(1,128)S(1)} %bitcast.380), channel_id=12, replica_groups=mesh['pair'=4,'src'=8,'tgt'=16] {'tgt'}, dimensions={0}, use_global_device_ids=true | all-gather | bytes 34816 | tf_op jit(solution)/shard_map/all_gather | solution.py:15
  247.8 9.8 %all-gather.44 = f32[8,1,256]{2,1,0:T(1,128)S(1)} all-gather(f32[1,1,256]{2,1,0:T(1,128)S(1)} %bitcast.389), channel_id=14, replica_groups=mesh['pair'=4,'src'=8,'tgt'=16] {'src'}, dimensions={0}, use_global_device_ids=true | all-gather | bytes 9216 | tf_op jit(solution)/shard_map/all_gather | solution.py:15
  257.6 11.4 %all-gather.45 = f32[8,1,256]{2,1,0:T(1,128)S(1)} all-gather(f32[1,1,256]{2,1,0:T(1,128)S(1)} %bitcast.406), channel_id=15, replica_groups=mesh['pair'=4,'src'=8,'tgt'=16] {'src'}, dimensions={0}, use_global_device_ids=true | all-gather | bytes 9216 | tf_op jit(solution)/shard_map/all_gather | solution.py:15
  269.8 22.8 %all-gather.47 = f32[16,1,512]{2,1,0:T(1,128)S(1)} all-gather(f32[1,1,512]{2,1,0:T(1,128)S(1)} %bitcast.396), channel_id=17, replica_groups=mesh['pair'=4,'src'=8,'tgt'=16] {'tgt'}, dimensions={0}, use_global_device_ids=true | all-gather | bytes 34816 | tf_op jit(solution)/shard_map/all_gather | solution.py:15
  293.2 15.0 %all-gather.46 = f32[16,1,512]{2,1,0:T(1,128)S(1)} all-gather(f32[1,1,512]{2,1,0:T(1,128)S(1)} %bitcast.381), channel_id=16, replica_groups=mesh['pair'=4,'src'=8,'tgt'=16] {'tgt'}, dimensions={0}, use_global_device_ids=true | all-gather | bytes 34816 | tf_op jit(solution)/shard_map/all_gather | solution.py:15
  310.7 9.8 %all-gather.48 = f32[8,1,256]{2,1,0:T(1,128)S(1)} all-gather(f32[1,1,256]{2,1,0:T(1,128)S(1)} %bitcast.390), channel_id=18, replica_groups=mesh['pair'=4,'src'=8,'tgt'=16] {'src'}, dimensions={0}, use_global_device_ids=true | all-gather | bytes 9216 | tf_op jit(solution)/shard_map/all_gather | solution.py:15
  320.5 11.4 %all-gather.49 = f32[8,1,256]{2,1,0:T(1,128)S(1)} all-gather(f32[1,1,256]{2,1,0:T(1,128)S(1)} %bitcast.407), channel_id=19, replica_groups=mesh['pair'=4,'src'=8,'tgt'=16] {'src'}, dimensions={0}, use_global_device_ids=true | all-gather | bytes 9216 | tf_op jit(solution)/shard_map/all_gather | solution.py:15
  332.6 22.8 %all-gather.51 = f32[16,1,512]{2,1,0:T(1,128)S(1)} all-gather(f32[1,1,512]{2,1,0:T(1,128)S(1)} %bitcast.397), channel_id=21, replica_groups=mesh['pair'=4,'src'=8,'tgt'=16] {'tgt'}, dimensions={0}, use_global_device_ids=true | all-gather | bytes 34816 | tf_op jit(solution)/shard_map/all_gather | solution.py:15
  355.5 15.0 %all-gather.50 = f32[16,1,512]{2,1,0:T(1,128)S(1)} all-gather(f32[1,1,512]{2,1,0:T(1,128)S(1)} %bitcast.382), channel_id=20, replica_groups=mesh['pair'=4,'src'=8,'tgt'=16] {'tgt'}, dimensions={0}, use_global_device_ids=true | all-gather | bytes 34816 | tf_op jit(solution)/shard_map/all_gather | solution.py:15
  371.7 9.8 %all-gather.52 = f32[8,1,256]{2,1,0:T(1,128)S(1)} all-gather(f32[1,1,256]{2,1,0:T(1,128)S(1)} %bitcast.391), channel_id=22, replica_groups=mesh['pair'=4,'src'=8,'tgt'=16] {'src'}, dimensions={0}, use_global_device_ids=true | all-gather | bytes 9216 | tf_op jit(solution)/shard_map/all_gather | solution.py:15
  381.5 11.4 %all-gather.53 = f32[8,1,256]{2,1,0:T(1,128)S(1)} all-gather(f32[1,1,256]{2,1,0:T(1,128)S(1)} %bitcast.408), channel_id=23, replica_groups=mesh['pair'=4,'src'=8,'tgt'=16] {'src'}, dimensions={0}, use_global_device_ids=true | all-gather | bytes 9216 | tf_op jit(solution)/shard_map/all_gather | solution.py:15
  393.6 22.8 %all-gather.55 = f32[16,1,512]{2,1,0:T(1,128)S(1)} all-gather(f32[1,1,512]{2,1,0:T(1,128)S(1)} %bitcast.398), channel_id=25, replica_groups=mesh['pair'=4,'src'=8,'tgt'=16] {'tgt'}, dimensions={0}, use_global_device_ids=true | all-gather | bytes 34816 | tf_op jit(solution)/shard_map/all_gather | solution.py:15
  416.5 15.0 %all-gather.54 = f32[16,1,512]{2,1,0:T(1,128)S(1)} all-gather(f32[1,1,512]{2,1,0:T(1,128)S(1)} %bitcast.383), channel_id=24, replica_groups=mesh['pair'=4,'src'=8,'tgt'=16] {'tgt'}, dimensions={0}, use_global_device_ids=true | all-gather | bytes 34816 | tf_op jit(solution)/shard_map/all_gather | solution.py:15
  432.7 9.8 %all-gather.56 = f32[8,1,256]{2,1,0:T(1,128)S(1)} all-gather(f32[1,1,256]{2,1,0:T(1,128)S(1)} %bitcast.392), channel_id=26, replica_groups=mesh['pair'=4,'src'=8,'tgt'=16] {'src'}, dimensions={0}, use_global_device_ids=true | all-gather | bytes 9216 | tf_op jit(solution)/shard_map/all_gather | solution.py:15
  442.6 11.4 %all-gather.57 = f32[8,1,256]{2,1,0:T(1,128)S(1)} all-gather(f32[1,1,256]{2,1,0:T(1,128)S(1)} %bitcast.409), channel_id=27, replica_groups=mesh['pair'=4,'src'=8,'tgt'=16] {'src'}, dimensions={0}, use_global_device_ids=true | all-gather | bytes 9216 | tf_op jit(solution)/shard_map/all_gather | solution.py:15
  454.7 22.8 %all-gather.59 = f32[16,1,512]{2,1,0:T(1,128)S(1)} all-gather(f32[1,1,512]{2,1,0:T(1,128)S(1)} %bitcast.399), channel_id=29, replica_groups=mesh['pair'=4,'src'=8,'tgt'=16] {'tgt'}, dimensions={0}, use_global_device_ids=true | all-gather | bytes 34816 | tf_op jit(solution)/shard_map/all_gather | solution.py:15
  477.5 15.0 %all-gather.58 = f32[16,1,512]{2,1,0:T(1,128)S(1)} all-gather(f32[1,1,512]{2,1,0:T(1,128)S(1)} %bitcast.384), channel_id=28, replica_groups=mesh['pair'=4,'src'=8,'tgt'=16] {'tgt'}, dimensions={0}, use_global_device_ids=true | all-gather | bytes 34816 | tf_op jit(solution)/shard_map/all_gather | solution.py:15
  493.7 9.8 %all-gather.60 = f32[8,1,256]{2,1,0:T(1,128)S(1)} all-gather(f32[1,1,256]{2,1,0:T(1,128)S(1)} %bitcast.386), channel_id=30, replica_groups=mesh['pair'=4,'src'=8,'tgt'=16] {'src'}, dimensions={0}, use_global_device_ids=true | all-gather | bytes 9216 | tf_op jit(solution)/shard_map/all_gather | solution.py:15
  503.6 11.4 %all-gather.61 = f32[8,1,256]{2,1,0:T(1,128)S(1)} all-gather(f32[1,1,256]{2,1,0:T(1,128)S(1)} %bitcast.403), channel_id=31, replica_groups=mesh['pair'=4,'src'=8,'tgt'=16] {'src'}, dimensions={0}, use_global_device_ids=true | all-gather | bytes 9216 | tf_op jit(solution)/shard_map/all_gather | solution.py:15
  515.7 22.8 %all-gather.63 = f32[16,1,512]{2,1,0:T(1,128)S(1)} all-gather(f32[1,1,512]{2,1,0:T(1,128)S(1)} %bitcast.400), channel_id=33, replica_groups=mesh['pair'=4,'src'=8,'tgt'=16] {'tgt'}, dimensions={0}, use_global_device_ids=true | all-gather | bytes 34816 | tf_op jit(solution)/shard_map/all_gather | solution.py:15
  538.5 15.0 %all-gather.62 = f32[16,1,512]{2,1,0:T(1,128)S(1)} all-gather(f32[1,1,512]{2,1,0:T(1,128)S(1)} %bitcast.385), channel_id=32, replica_groups=mesh['pair'=4,'src'=8,'tgt'=16] {'tgt'}, dimensions={0}, use_global_device_ids=true | all-gather | bytes 34816 | tf_op jit(solution)/shard_map/all_gather | solution.py:15
  556.3 52.7 %reduce-scatter.5.cloned.1.call-done = f32[40,32]{0,1:T(8,128)} async-done(((f32[40,512]{0,1:T(8,128)}), f32[40,32]{0,1:T(8,128)}) %reduce-scatter.5.cloned.1.call-update) | async-done | bytes 5136 | tf_op jit(solution)/shard_map/reduce_scatter | solution.py:118
  609.7 1.5 collective-permute-start.1
  611.2 2.9 collective-permute-done.1
  614.1 54.4 %all_gather.265 = bf16[40,4096]{0,1:T(8,128)(2,1)S(1)} all-gather(bf16[40,32]{0,1:T(8,128)(2,1)S(1)} %collective-permute-done.1), channel_id=1, replica_groups=mesh['pair'=4,'src'=8,'tgt'=16] {'src','tgt'}, dimensions={1}, use_global_device_ids=true | all-gather | bytes 330240 | tf_op jit(solution)/shard_map/all_gather | solution.py:123
  669.6 52.1 %reduce-scatter.7.cloned.1.call-done = f32[40,32]{0,1:T(8,128)} async-done(((f32[40,512]{0,1:T(8,128)}), f32[40,32]{0,1:T(8,128)}) %reduce-scatter.7.cloned.1.call-update) | async-done | bytes 5136 | tf_op jit(solution)/shard_map/reduce_scatter | solution.py:118
  722.5 1.3 collective-permute-start.2
  723.8 3.1 collective-permute-done.2
  726.9 54.5 %all_gather.266 = bf16[40,4096]{0,1:T(8,128)(2,1)S(1)} all-gather(bf16[40,32]{0,1:T(8,128)(2,1)S(1)} %collective-permute-done.2), channel_id=1, replica_groups=mesh['pair'=4,'src'=8,'tgt'=16] {'src','tgt'}, dimensions={1}, use_global_device_ids=true | all-gather | bytes 330240 | tf_op jit(solution)/shard_map/all_gather | solution.py:123
  782.5 52.1 %reduce-scatter.9.cloned.1.call-done = f32[40,32]{0,1:T(8,128)} async-done(((f32[40,512]{0,1:T(8,128)}), f32[40,32]{0,1:T(8,128)}) %reduce-scatter.9.cloned.1.call-update) | async-done | bytes 5136 | tf_op jit(solution)/shard_map/reduce_scatter | solution.py:118
  835.3 1.3 collective-permute-start.3
  836.6 3.1 collective-permute-done.3
  839.7 54.6 %all_gather.267 = bf16[40,4096]{0,1:T(8,128)(2,1)S(1)} all-gather(bf16[40,32]{0,1:T(8,128)(2,1)S(1)} %collective-permute-done.3), channel_id=1, replica_groups=mesh['pair'=4,'src'=8,'tgt'=16] {'src','tgt'}, dimensions={1}, use_global_device_ids=true | all-gather | bytes 330240 | tf_op jit(solution)/shard_map/all_gather | solution.py:123
  895.9 51.5 %reduce-scatter.11.cloned.1.call-done = f32[40,32]{0,1:T(8,128)} async-done(((f32[40,512]{0,1:T(8,128)}), f32[40,32]{0,1:T(8,128)}) %reduce-scatter.11.cloned.1.call-update) | async-done | bytes 5136 | tf_op jit(solution)/shard_map/reduce_scatter | solution.py:118
  947.4 1.4 select_bitcast_fusion
  (560 shorter events, 45.5 us)
Async XLA Ops:
  7.2 601.8 %reduce-scatter.5.cloned.1.call-start = ((), (), s32[]{:S(2)}) async-start(), calls=%async_computation.4 | async-start | bytes 278528 | tf_op jit(solution)/shard_map/reduce_scatter | solution.py:118
  8.0 1.4 copy-start
  8.0 6.3 collective-permute-start
  9.5 2.7 copy-start.16
  9.6 0.7 copy-start.18
  12.3 0.7 copy-start.19
  14.4 30.2 %copy-start.17 = (f32[30,256]{1,0:T(8,128)S(1)}, f32[30,256]{1,0:T(8,128)}, u32[]{:S(2)}) copy-start(f32[30,256]{1,0:T(8,128)} %param.38) | copy-start | bytes 92164
  55.5 0.6 copy-start.12
  67.3 0.6 copy-start.14
  67.9 0.7 slice-start.10
  67.9 0.7 slice-start.8
  102.1 0.6 copy-start.1
  117.7 0.6 copy-start.2
  118.3 0.7 slice-start.1
  118.3 0.7 slice-start
  130.0 0.6 copy-start.13
  142.0 0.6 copy-start.15
  142.6 0.7 slice-start.11
  142.6 0.7 slice-start.9
  166.8 0.6 copy-start.3
  182.4 0.6 copy-start.4
  183.0 0.7 slice-start.3
  183.0 0.7 slice-start.2
  229.7 0.6 copy-start.5
  245.3 0.6 copy-start.6
  245.9 0.7 slice-start.5
  245.9 0.7 slice-start.4
  292.6 0.6 copy-start.7
  308.2 0.6 copy-start.8
  308.8 0.7 slice-start.7
  308.8 0.7 slice-start.6
  555.6 166.2 %reduce-scatter.7.cloned.1.call-start = ((), (), s32[]{:S(2)}) async-start(), calls=%async_computation.5 | async-start | bytes 278528 | tf_op jit(solution)/shard_map/reduce_scatter | solution.py:118
  609.7 4.4 collective-permute-start.1
  669.6 165.0 %reduce-scatter.9.cloned.1.call-start = ((), (), s32[]{:S(2)}) async-start(), calls=%async_computation.6 | async-start | bytes 278528 | tf_op jit(solution)/shard_map/reduce_scatter | solution.py:118
  722.5 4.4 collective-permute-start.2
  782.4 165.0 %reduce-scatter.11.cloned.1.call-start = ((), (), s32[]{:S(2)}) async-start(), calls=%async_computation.7 | async-start | bytes 278528 | tf_op jit(solution)/shard_map/reduce_scatter | solution.py:118
  835.3 4.4 collective-permute-start.3
  895.3 52.1 %copy-start.9 = (f32[40,32]{0,1:T(8,128)S(1)}, f32[40,32]{0,1:T(8,128)}, u32[]{:S(2)}) copy-start(f32[40,32]{0,1:T(8,128)} %reduce-scatter.5.cloned.1.call-done) | copy-start | bytes 15364
  895.3 52.1 %copy-start.10 = (f32[40,32]{0,1:T(8,128)S(1)}, f32[40,32]{0,1:T(8,128)}, u32[]{:S(2)}) copy-start(f32[40,32]{0,1:T(8,128)} %reduce-scatter.7.cloned.1.call-done) | copy-start | bytes 15364
  895.3 52.1 %copy-start.11 = (f32[40,32]{0,1:T(8,128)S(1)}, f32[40,32]{0,1:T(8,128)}, u32[]{:S(2)}) copy-start(f32[40,32]{0,1:T(8,128)} %reduce-scatter.9.cloned.1.call-done) | copy-start | bytes 15364
Sparse Core Ops, SparseCore 0:
  555.7 53.2 reduce-scatter.4
  669.7 51.9 reduce-scatter.6
  782.5 51.9 reduce-scatter.8
  895.5 51.9 reduce-scatter.10
where the time goes:
time: 958 us; the launch traced here: 955 us
  blocking collectives  675 us (70%)
  waiting for transfers between devices  217 us (23%)
  local copies, waits for them, and re-layouts  16.2 us (2%)
  other arithmetic  16.1 us (2%)
  between operations  15.7 us (2%)
    all_gather x32, blocking collectives, joined(): everything = jax.tree.map(lambda part: lax.all_gather(part, axis), shard)  482 us
    reduce_scatter x4, waiting for transfers between devices, local(): lax.psum_scatter(partial_value, 'tgt', scatter_dimension=1, tiled=True)  208 us
    all_gather x3, blocking collectives, local(): gathered = lax.all_gather(passed, ('src', 'tgt'), axis=1, tiled=True)  164 us
    psum x1, blocking collectives, from_root(): return lax.psum(jnp.where(mine, shard, jnp.zeros_like(shard)), axis)  30.1 us
  transfers between devices with their start and end apart: 8, of which 7 were waited for; matrix products, arithmetic and copies ran while one was open for 0% of the time, Pallas kernels for 0%

commit v1 on v0

v1 whole, which is shorter than its diff:
```python
import functools
import math

import jax
import jax.numpy as jnp
from jax import lax
from jax.experimental import pallas as pl
from jax.experimental.pallas import tpu as pltpu
from jax.sharding import PartitionSpec as P

MESH = pl.DeviceIdType.MESH
F32 = jnp.float32
BF16 = jnp.bfloat16

ITERS = 8
EPS = 0.1
LAM = 1.0
NEG = -1e30
SHRINK = LAM / (LAM + EPS)
LOG2E = 1.0 / math.log(2.0)
COST_SCALE = LOG2E / (EPS * 60.0)
LOWEST = -3e38

HALF = 2048
QUARTER = 1024
LANES = 128


def lane_iota():
    return lax.broadcasted_iota(jnp.int32, (8, LANES), 1)


def sub_iota():
    return lax.broadcasted_iota(jnp.int32, (8, LANES), 0)


def spread_columns(packed, dst, base):
    def body(k, carry):
        turned = pltpu.roll(packed, lax.rem(LANES - 32 * k, LANES), axis=1)
        for t in range(32):
            row = pl.multiple_of(base + (32 * k + t) * 8, 8)
            dst[pl.ds(row, 8), :] = jnp.broadcast_to(turned[:, t : t + 1], (8, LANES))
        return carry

    lax.fori_loop(0, LANES // 32, body, 0)


def lse_pass(cost, spread, rows, tiles, group):
    def walk(start, update):
        def body(k, acc):
            acc = list(acc)
            for t in range(group):
                row = pl.multiple_of((k * group + t) * 8, 8)
                left = spread[pl.ds(row, 8), :]
                for q in range(tiles):
                    acc[q] = update(q, acc[q], left - cost[pl.ds(row, 8), LANES * q : LANES * (q + 1)])
            return tuple(acc)

        return lax.fori_loop(0, rows // (8 * group), body, tuple(start))

    peaks = walk([jnp.full((8, LANES), LOWEST, F32)] * tiles, lambda q, a, s: jnp.maximum(a, s))
    peaks = [jnp.broadcast_to(jnp.max(a, axis=0, keepdims=True), (8, LANES)) for a in peaks]
    sums = walk([jnp.zeros((8, LANES), F32)] * tiles, lambda q, a, s: a + jnp.exp2(s - peaks[q]))
    sums = [jnp.broadcast_to(jnp.sum(a, axis=0, keepdims=True), (8, LANES)) for a in sums]
    which = sub_iota()
    out = []
    for r in range(tiles // 8):
        m, s = peaks[8 * r], sums[8 * r]
        for q in range(1, 8):
            m = jnp.where(which == q, peaks[8 * r + q], m)
            s = jnp.where(which == q, sums[8 * r + q], s)
        out.append((m, s))
    return out


def three_parts(x):
    high = x.astype(BF16).astype(F32)
    rest = x - high
    mid = rest.astype(BF16).astype(F32)
    low = (rest - mid).astype(BF16).astype(F32)
    return high, mid, low


def kernel(
    src_ref, fin_ref, growth_ref, live_ref, fates_ref, out_ref, pot_ref,
    xst, fst, fates_st, xbuf, ybuf, xk, xt0, xt1, yt, yts, ct, cr, ub, vb, wt,
    csend, cslot, rsend, rslot, fsend, fother, hand, pbuf, pbf, chin, s1, s2st, s2,
    in_send, x_sem, y_sem, f_sem, fs_send, cs_send, cs_recv, rs_send, rs_recv,
    p_send, p_recv, ch_send, ch_recv, s1_send, s1_recv, s2_send, s2_recv,
):
    p = lax.axis_index("pair")
    z = lax.axis_index("src")
    t = lax.axis_index("tgt")
    y, c = t // 2, t % 2
    zb, yb = z % 2, y % 2
    b = 2 * zb + yb
    z0, y0 = z - zb, y - yb
    a, d = z // 2, y // 2
    home = z // 4
    last = p == 3

    def at(pp, zz, yy, cc):
        return {"pair": pp, "src": zz, "tgt": 2 * yy + cc}

    def push(src, dst, send, recv, where):
        return pltpu.make_async_remote_copy(src, dst, send, recv, device_id=where, device_id_type=MESH)

    def same(pp, zz, yy, cc):
        return (pp == p) & (zz == z) & (yy == y) & (cc == c)

    up, down = jnp.minimum(p + 1, 3), jnp.maximum(p - 1, 0)
    chips = [((b + k) % 4) for k in range(1, 4)]
    chip_at = lambda bb: (z0 + bb // 2, y0 + bb % 2)
    core_peer = (p, z, y, 1 - c)
    row_peers = [(p, *chip_at(bb), c) for bb in chips]
    x_to = [(c == home, (p, (z + k) % 8, y, c)) for k in range(1, 8)]
    x_from = [(4 * c + k != z, (p, 4 * c + k, y, c)) for k in range(4)]
    y_active = (p > 0) & (yb == a % 2)
    y_to = [(y_active, (down, home + 2 * k, y, c)) for k in range(4)]
    y_from = [(p < 3, (up, 2 * b + k, y, c)) for k in range(2)]
    f_active = last & (zb == y // 4)
    f_to = [(p, z, d % 2 + 2 * (k // 2), k % 2) for k in range(8)]
    f_from = [(p, z, 2 * b + k // 2, k % 2) for k in range(4)]
    ch_to = [(p > 0, (down, *chip_at(2 * c + k // 2), k % 2)) for k in range(4)]
    ch_from = [(p < 3, (up, *chip_at(k), b // 2)) for k in range(4)]
    s1_to = [(p, z0 + k // 4, y0 + (k % 4) // 2, k % 2) for k in range(8)]
    s1_from = [(p, *chip_at(k), home) for k in range(4)]
    quad = 2 * yb + c
    s2_to = [(p, z, 2 * quad + k // 2, k % 2) for k in range(4)]
    s2_from = [(p, z, 2 * k + d // 2, d % 2) for k in range(4)]

    barrier = pltpu.get_barrier_semaphore()
    expected = jnp.int32(4)

    def greet(cond, where):
        @pl.when(cond)
        def _():
            pl.semaphore_signal(barrier, inc=1, device_id=at(*where), device_id_type=MESH)

    pl.semaphore_signal(barrier, inc=1, device_id=at(*core_peer), device_id_type=MESH)
    for where in row_peers:
        pl.semaphore_signal(barrier, inc=1, device_id=at(*where), device_id_type=MESH)
    for cond, where in x_from + y_from + ch_from:
        greet(cond, where)
    for where in f_from:
        greet(last & jnp.logical_not(same(*where)), where)
    for where in s1_from + s2_from:
        greet(jnp.logical_not(same(*where)), where)
    for cond, where in x_to + y_to + ch_to:
        expected = expected + jnp.where(cond, 1, 0)
    for where in f_to:
        expected = expected + jnp.where(f_active & jnp.logical_not(same(*where)), 1, 0)
    for where in s1_to:
        expected = expected + jnp.where((c == home) & jnp.logical_not(same(*where)), 1, 0)
    for where in s2_to:
        expected = expected + jnp.where(jnp.logical_not(same(*where)), 1, 0)

    xst[30:32, :] = jnp.zeros((2, 512), F32)
    xst[0:30, :] = src_ref[0]
    xst[30:31, :] = growth_ref[...]
    fst[...] = jnp.zeros_like(fst)
    fst[0:30, :] = fin_ref[...]
    for g in range(4):
        block = jnp.concatenate([fates_ref[10 * g : 10 * g + 10, :], jnp.zeros((6, 256), F32)], axis=0)
        fates_st[g] = block.astype(BF16)

    pl.semaphore_wait(barrier, expected)

    for k, (cond, where) in enumerate(x_to):
        @pl.when(cond)
        def _(where=where):
            push(xst, xbuf.at[z % 4], in_send, x_sem, at(*where)).start()

    @pl.when(c == home)
    def _():
        pltpu.make_async_copy(xst, xbuf.at[z % 4], x_sem).start()

    for cond, where in y_to:
        @pl.when(cond)
        def _(where=where):
            push(xst, ybuf.at[zb], in_send, y_sem, at(*where)).start()

    slot = t % 4
    fin_dst = ybuf.at[slot // 2, :, pl.ds(pl.multiple_of((slot % 2) * 256, 256), 256)]
    fate_dst = hand.at[:, pl.ds(pl.multiple_of(slot * 256, 256), 256)]
    for where in f_to:
        mine = same(*where)

        @pl.when(f_active & jnp.logical_not(mine))
        def _(where=where):
            push(fst, fin_dst, fs_send, y_sem, at(*where)).start()
            push(fates_st.at[where[2] // 2], fate_dst, fs_send, f_sem, at(*where)).start()

        @pl.when(f_active & mine)
        def _(where=where):
            pltpu.make_async_copy(fst, fin_dst, y_sem).start()
            pltpu.make_async_copy(fates_st.at[where[2] // 2], fate_dst, f_sem).start()

    live_now = jnp.int32(0)
    live_next = jnp.int32(0)
    for k in range(4):
        live_now = live_now + jnp.where(p == k, live_ref[k], 0)
        live_next = live_next + jnp.where(p == k, live_ref[k + 1], 0)
    log_now = jnp.log2(jnp.broadcast_to(live_now.astype(F32), (8, LANES)))
    log_next = jnp.log2(jnp.broadcast_to(live_next.astype(F32), (8, LANES)))
    lanes, subs = lane_iota(), sub_iota()
    row_ids = [HALF * c + LANES * (8 * r + subs) + lanes for r in range(2)]
    col_ids = QUARTER * b + 8 * lanes + subs
    log_b = jnp.where(col_ids < live_next, -log_next, NEG)

    pltpu.make_async_copy(ybuf, ybuf, y_sem).wait()
    keep = lax.broadcasted_iota(jnp.int32, (32, 512), 0) < 30
    for k in range(2):
        cells = jnp.where(keep, ybuf[k], 0.0)
        high, mid, low = three_parts(-2.0 * cells)
        stack = jnp.concatenate([high, mid, low, high], axis=0)
        yt[512 * k : 512 * (k + 1), :] = jnp.transpose(stack)

    for sub in range(8):
        yts[LANES * sub : LANES * (sub + 1), :] = yt[pl.ds(sub, LANES, stride=8), :].astype(BF16)

    def y_norms(k, packed):
        for j in range(16):
            row = pl.multiple_of((16 * k + j) * 8, 8)
            tile = yt[pl.ds(row, 8), :]
            whole = tile + pltpu.roll(tile, 96, axis=1) + pltpu.roll(tile, 64, axis=1)
            whole = jnp.where(lanes < 32, whole, 0.0)
            norm = jnp.broadcast_to(0.25 * jnp.sum(whole * whole, axis=1, keepdims=True), (8, LANES))
            vb[pl.ds(row, 8), :] = norm
            packed = jnp.where(lanes == 16 * k + j, norm, packed)
        return packed

    y_sq = lax.fori_loop(0, 8, y_norms, jnp.zeros((8, LANES), F32))

    pltpu.make_async_copy(xbuf, xbuf, x_sem).wait()
    x_rows = []
    g_rows = []
    for k in range(4):
        cells = jnp.where(keep, xbuf[k], 0.0)
        norms = jnp.sum(cells * cells, axis=0, keepdims=True)
        x_rows += [norms[:, LANES * q : LANES * (q + 1)] for q in range(4)]
        g_rows += [xbuf[k, 30:31, LANES * q : LANES * (q + 1)] for q in range(4)]
        high, mid, low = three_parts(cells)
        none = jnp.zeros_like(high)
        for part, stack in enumerate(([high, high, high, none], [mid, mid, none, low])):
            stack = jnp.concatenate(stack, axis=0)
            xk[LANES * part : LANES * (part + 1), 512 * k : 512 * (k + 1)] = stack.astype(BF16)
            turned = jnp.transpose(stack)
            for q in range(4):
                first = 1024 * (k // 2) + 4 * (k % 2) + q
                (xt0, xt1)[part][pl.ds(first, LANES, stride=8), :] = turned[LANES * q : LANES * (q + 1), :]
    x_sq = [jnp.concatenate(x_rows[8 * r : 8 * r + 8], axis=0) for r in range(2)]
    grown = [jnp.concatenate(g_rows[8 * r : 8 * r + 8], axis=0) for r in range(2)]
    log_a = [jnp.where(row_ids[r] < live_now, jnp.log2(grown[r]) - log_now, NEG) for r in range(2)]
    for r in range(2):
        spread_columns(x_sq[r], ub, 1024 * r)

    def ct_rows(k, carry):
        row = pl.multiple_of(k * 128, 128)
        left = yt[pl.ds(row, 128), :].astype(BF16)
        left = jnp.concatenate([left, left], axis=1)
        cross = jnp.dot(left, xk[...], preferred_element_type=F32)
        for q in range(16):
            norm = vb[pl.ds(row, 128), :] + x_rows[q]
            ct[pl.ds(row, 128), LANES * q : LANES * (q + 1)] = (
                norm + cross[:, LANES * q : LANES * (q + 1)]
            ) * COST_SCALE
        return carry

    lax.fori_loop(0, 8, ct_rows, 0)

    def cr_rows(k, carry):
        row = pl.multiple_of(k * 128, 128)
        left = jnp.concatenate([xt0[pl.ds(row, 128), :], xt1[pl.ds(row, 128), :]], axis=1).astype(BF16)
        right = yts[...]
        right = jnp.concatenate([right, right], axis=1)
        cross = lax.dot_general(left, right, (((1,), (1,)), ((), ())), preferred_element_type=F32)
        for q in range(8):
            norm = ub[pl.ds(row, 128), :] + y_sq[q : q + 1, :]
            cr[pl.ds(row, 128), LANES * q : LANES * (q + 1)] = (
                norm + cross[:, LANES * q : LANES * (q + 1)]
            ) * COST_SCALE
        return carry

    lax.fori_loop(0, 16, cr_rows, 0)

    for r in range(2):
        spread_columns(log_a[r], ub, 1024 * r)

    def iterate(step, carry):
        par = step % 2
        ((m0, s0),) = lse_pass(cr, ub, HALF, 8, 8)
        csend[par, 0:8] = m0
        csend[par, 8:16] = s0
        copy = push(csend.at[par], cslot.at[par], cs_send.at[par], cs_recv.at[par], at(*core_peer))
        copy.start()
        copy.wait()
        m1, s1_ = cslot[par, 0:8], cslot[par, 8:16]
        peak = jnp.maximum(m0, m1)
        total = s0 * jnp.exp2(m0 - peak) + s1_ * jnp.exp2(m1 - peak)
        pot_v = -SHRINK * (peak + jnp.log2(total)) + log_b
        spread_columns(pot_v, vb, 0)
        rows = lse_pass(ct, vb, QUARTER, 16, 4)
        for r in range(2):
            rsend[par, 8 * r : 8 * r + 8] = rows[r][0]
            rsend[par, 16 + 8 * r : 24 + 8 * r] = rows[r][1]
        rslot[par, b] = rsend[par]
        copies = [
            push(rsend.at[par], rslot.at[par, b], rs_send.at[par], rs_recv.at[par], at(*where))
            for where in row_peers
        ]
        for copy in copies:
            copy.start()
        three = rslot.at[par, pl.ds(0, 3)]
        pltpu.make_async_copy(three, three, rs_recv.at[par]).wait()
        out = []
        for r in range(2):
            ms = [rslot[par, k, 8 * r : 8 * r + 8] for k in range(4)]
            ss = [rslot[par, k, 16 + 8 * r : 24 + 8 * r] for k in range(4)]
            peak = jnp.maximum(jnp.maximum(ms[0], ms[1]), jnp.maximum(ms[2], ms[3]))
            total = ss[0] * jnp.exp2(ms[0] - peak)
            for k in range(1, 4):
                total = total + ss[k] * jnp.exp2(ms[k] - peak)
            level = -SHRINK * (peak + jnp.log2(total))
            spread_columns(level + log_a[r], ub, 1024 * r)
            out += [peak, total, level]
        pltpu.make_async_copy(three, three, rs_send.at[par]).wait()
        return tuple(out)

    zero = jnp.zeros((8, LANES), F32)
    final = lax.fori_loop(0, ITERS, iterate, (zero,) * 6)

    for r in range(2):
        fsend[8 * r : 8 * r + 8] = final[3 * r + 2] * (EPS / LOG2E)
    pot_copy = push(fsend, fother, p_send, p_recv, at(*core_peer))
    pot_copy.start()

    wpeak = []
    wscale = []
    for r in range(2):
        inv = 1.0 / final[3 * r + 1]
        for q in range(8):
            wpeak.append(final[3 * r][q : q + 1, :])
            wscale.append(inv[q : q + 1, :])

    def w_rows(k, carry):
        row = pl.multiple_of(k * 16, 16)
        left = vb[pl.ds(row, 16), :]
        for q in range(16):
            s = left - ct[pl.ds(row, 16), LANES * q : LANES * (q + 1)]
            w = jnp.exp2(s - wpeak[q]) * wscale[q]
            wt[pl.ds(row, 16), LANES * q : LANES * (q + 1)] = w.astype(BF16)
        return carry

    lax.fori_loop(0, QUARTER // 16, w_rows, 0)

    @pl.when(last)
    def _():
        pltpu.make_async_copy(hand, hand, f_sem).wait()

    @pl.when(jnp.logical_not(last))
    def _():
        pltpu.make_async_copy(chin, chin, ch_recv).wait()
        total = chin[0].astype(F32)
        for k in range(1, 4):
            total = total + chin[k].astype(F32)
        hand[...] = total.astype(BF16)

    ids = HALF * c + lax.broadcasted_iota(jnp.int32, (16, HALF), 1)
    part = jnp.dot(hand[...], wt[...], preferred_element_type=F32)
    part = jnp.where(ids < live_now, part, 0.0)
    pbuf[...] = part
    pbf[0] = part[:, 0:QUARTER].astype(BF16)
    pbf[1] = part[:, QUARTER:HALF].astype(BF16)
    for k, (cond, where) in enumerate(ch_to):
        @pl.when(cond)
        def _(k=k, where=where):
            push(pbf.at[k // 2], chin.at[b], ch_send, ch_recv, at(*where)).start()

    def s1_src(k):
        first = pl.multiple_of(QUARTER * (a % 2) + LANES * k, LANES)
        return pbuf.at[:, pl.ds(first, LANES)]

    for k, where in enumerate(s1_to):
        mine = same(*where)

        @pl.when((c == home) & jnp.logical_not(mine))
        def _(k=k, where=where):
            push(s1_src(k), s1.at[b], s1_send, s1_recv, at(*where)).start()

        @pl.when((c == home) & mine)
        def _(k=k):
            pltpu.make_async_copy(s1_src(k), s1.at[b], s1_recv).start()

    pltpu.make_async_copy(s1, s1, s1_recv).wait()
    s2st[...] = (s1[0] + s1[1]) + (s1[2] + s1[3])
    for where in s2_to:
        mine = same(*where)

        @pl.when(jnp.logical_not(mine))
        def _(where=where):
            push(s2st, s2.at[d], s2_send, s2_recv, at(*where)).start()

        @pl.when(mine)
        def _():
            pltpu.make_async_copy(s2st, s2.at[d], s2_recv).start()

    pot_copy.wait()
    own = jnp.where(c == home, fsend[...], fother[...])
    picked = own[0:4]
    for k in range(1, 4):
        picked = jnp.where(z % 4 == k, own[4 * k : 4 * k + 4], picked)
    for k in range(4):
        pot_ref[0:1, LANES * k : LANES * (k + 1)] = picked[k : k + 1]

    pltpu.make_async_copy(s2, s2, s2_recv).wait()
    turn = lax.rem(LANES - 32 * quad, LANES)
    for g in range(4):
        out_ref[0, 10 * g : 10 * g + 10, :] = pltpu.roll(s2[g], turn, axis=1)[0:10, 0:32]

    def settle(cond, ref, sem):
        @pl.when(cond)
        def _():
            pltpu.make_async_copy(ref, ref, sem).wait()

    for cond, where in x_to + y_to:
        settle(cond, xst, in_send)
    for where in f_to:
        off = f_active & jnp.logical_not(same(*where))
        settle(off, fst, fs_send)
        settle(off, fates_st.at[0], fs_send)
    for cond, where in ch_to:
        settle(cond, pbf.at[0], ch_send)
    for where in s1_to:
        settle((c == home) & jnp.logical_not(same(*where)), s2st, s1_send)
    for where in s2_to:
        settle(jnp.logical_not(same(*where)), s2st, s2_send)


def local(src_cells, final_cells, growth, live, final_fates):
    vmem = pl.BlockSpec(memory_space=pltpu.VMEM)
    dma = pltpu.SemaphoreType.DMA
    V = pltpu.VMEM
    return tuple(pl.pallas_call(
        kernel,
        out_shape=(
            jax.ShapeDtypeStruct((1, 40, 32), F32),
            jax.ShapeDtypeStruct((1, 512), F32),
        ),
        in_specs=[vmem, vmem, vmem, pl.BlockSpec(memory_space=pltpu.SMEM), vmem],
        out_specs=(vmem, vmem),
        scratch_shapes=[
            V((32, 512), F32), V((32, 256), F32), V((4, 16, 256), BF16),
            V((4, 32, 512), F32), V((2, 32, 512), F32),
            V((256, HALF), BF16), V((HALF, 128), F32), V((HALF, 128), F32), V((QUARTER, 128), F32), V((QUARTER, 128), BF16),
            V((QUARTER, HALF), F32), V((HALF, QUARTER), F32),
            V((HALF, 128), F32), V((QUARTER, 128), F32), V((QUARTER, HALF), BF16),
            V((2, 16, 128), F32), V((2, 16, 128), F32), V((2, 32, 128), F32), V((2, 4, 32, 128), F32),
            V((16, 128), F32), V((16, 128), F32),
            V((16, QUARTER), BF16), V((16, HALF), F32), V((2, 16, QUARTER), BF16), V((4, 16, QUARTER), BF16),
            V((4, 16, 128), F32), V((16, 128), F32), V((4, 16, 128), F32),
            dma(()), dma(()), dma(()), dma(()), dma(()), dma((2,)), dma((2,)), dma((2,)), dma((2,)),
            dma(()), dma(()), dma(()), dma(()), dma(()), dma(()), dma(()), dma(()),
        ],
        compiler_params=pltpu.CompilerParams(
            collective_id=0, has_side_effects=True, vmem_limit_bytes=48 * 2**20
        ),
        name="transport",
    )(src_cells, final_cells, growth, live, final_fates))


def solution(mesh):
    placed = (P("pair", None, "src"), P(None, "tgt"), P("pair", "src"), P(), P(None, "tgt"))
    return jax.shard_map(
        local,
        mesh=mesh,
        in_specs=placed,
        out_specs=(P("pair", None, ("src", "tgt")), P("pair", "src")),
        check_vma=False,
    )
```

time: 958 us -> 156 us (0.16)
  blocking collectives: 675 us -> 0 us
  waiting for transfers between devices: 217 us -> 0 us
  Pallas kernels: 0 us -> 153 us
  other arithmetic: 16.1 us -> 0 us
  between operations: 15.7 us -> 0.69 us
  local copies, waits for them, and re-layouts: 16.2 us -> 2.14 us
    all_gather x35 -> x0, blocking collectives: 645 us -> none  [the longest x32 482 us: joined(): everything = jax.tree.map(lambda part: lax.all_gather(part, axis), shard)]
    reduce_scatter x4 -> x0, waiting for transfers between devices: 208 us -> none  [local(): lax.psum_scatter(partial_value, 'tgt', scatter_dimension=1, tiled=True)]
    pallas_call x0 -> x1, Pallas kernels: none -> 153 us  [local(): pl.pallas_call(kernel, out_shape=(jax.ShapeDtypeStruct((1, 40, 32), F32),...]
    psum x1 -> x0, blocking collectives: 30.1 us -> none  [from_root(): return lax.psum(jnp.where(mine, shard, jnp.zeros_like(shard)), axis)]
  transfers between devices with their start and end apart: 8 -> 0, of which waited for: 7 -> 0; matrix products, arithmetic and copies ran while one was open for 0% -> 0% of each run, Pallas kernels for 0% -> 0%
where the time goes in v1:
time: 156 us
  Pallas kernels  153 us (98%)
  local copies, waits for them, and re-layouts  2.14 us (1%)
    pallas_call x1, Pallas kernels, local(): pl.pallas_call(kernel, out_shape=(jax.ShapeDtypeStruct((1, 40, 32), F32),...  153 us

profile of v1, /device:TPU:1, one launch (start us, length us, event | category | flops | bytes accessed | tf_op | source)
XLA Modules:
  0.0 155.6 jit_solution(1232660307171747228)
XLA Ops:
  0.6 0.0 copy-start
  0.6 0.0 copy-start.3
  0.7 0.0 copy-start.2
  0.7 0.0 copy-start.1
  0.7 0.9 copy.7.src_ref
  1.5 0.0 copy-done
  1.5 0.0 copy-done.3
  1.5 0.0 copy-done.2
  1.6 0.0 copy-done.1
  1.6 152.8 %transport.1 = (f32[1,40,32]{2,1,0:T(8,128)S(1)}, f32[1,512]{1,0:T(1,128)S(1)}) custom-call(f32[1,30,512]{2,1,0:T(8,128)S(1)} %copy.7.src_ref, f32[30,256]{1,0:T(8,128)S(1)} %copy-done.1, f32[1,512]{1,0:T(1,128)S(1)} %copy-done.2, s32[5]{0:T(128)S(1)} %copy-done.3, f32[40,256]{1,0:T(8,128)S(1)} %copy-done), custom_call_target="tpu_custom_call" | custom-call | tf_op jit(solution)/shard_map/transport/pallas_call | solution.py:444
  154.4 0.7 copy.8
  155.1 0.6 copy.10
Async XLA Ops:
  0.6 0.9 copy-start
  0.6 0.9 copy-start.3
  0.7 0.9 copy-start.2
  0.7 0.9 copy-start.1

commit v2 on v1

--- a/solution.py
+++ b/solution.py
@@ -24,6 +24,7 @@
 HALF = 2048
 QUARTER = 1024
 LANES = 128
+GROUP = 32
 
 
 def lane_iota():
@@ -35,42 +36,37 @@
 
 
 def spread_columns(packed, dst, base):
-    def body(k, carry):
-        turned = pltpu.roll(packed, lax.rem(LANES - 32 * k, LANES), axis=1)
-        for t in range(32):
-            row = pl.multiple_of(base + (32 * k + t) * 8, 8)
-            dst[pl.ds(row, 8), :] = jnp.broadcast_to(turned[:, t : t + 1], (8, LANES))
-        return carry
-
-    lax.fori_loop(0, LANES // 32, body, 0)
-
-
-def lse_pass(cost, spread, rows, tiles, group):
+    for t in range(LANES):
+        row = pl.multiple_of(base + 8 * t, 8)
+        dst[pl.ds(row, 8), :] = jnp.broadcast_to(packed[:, t : t + 1], (8, LANES))
+
+
+def lse_pass(cost, spread, row0, lane0):
+    tiles = 8
+
     def walk(start, update):
         def body(k, acc):
             acc = list(acc)
-            for t in range(group):
-                row = pl.multiple_of((k * group + t) * 8, 8)
+            for t in range(GROUP):
+                row = pl.multiple_of(row0 + (k * GROUP + t) * 8, 8)
                 left = spread[pl.ds(row, 8), :]
                 for q in range(tiles):
-                    acc[q] = update(q, acc[q], left - cost[pl.ds(row, 8), LANES * q : LANES * (q + 1)])
+                    lane = pl.multiple_of(lane0 + LANES * q, LANES)
+                    acc[q] = update(q, acc[q], left - cost[pl.ds(row, 8), pl.ds(lane, LANES)])
             return tuple(acc)
 
-        return lax.fori_loop(0, rows // (8 * group), body, tuple(start))
+        return lax.fori_loop(0, QUARTER // (8 * GROUP), body, tuple(start))
 
     peaks = walk([jnp.full((8, LANES), LOWEST, F32)] * tiles, lambda q, a, s: jnp.maximum(a, s))
     peaks = [jnp.broadcast_to(jnp.max(a, axis=0, keepdims=True), (8, LANES)) for a in peaks]
     sums = walk([jnp.zeros((8, LANES), F32)] * tiles, lambda q, a, s: a + jnp.exp2(s - peaks[q]))
     sums = [jnp.broadcast_to(jnp.sum(a, axis=0, keepdims=True), (8, LANES)) for a in sums]
     which = sub_iota()
-    out = []
-    for r in range(tiles // 8):
-        m, s = peaks[8 * r], sums[8 * r]
-        for q in range(1, 8):
-            m = jnp.where(which == q, peaks[8 * r + q], m)
-            s = jnp.where(which == q, sums[8 * r + q], s)
-        out.append((m, s))
-    return out
+    m, s = peaks[0], sums[0]
+    for q in range(1, 8):
+        m = jnp.where(which == q, peaks[q], m)
+        s = jnp.where(which == q, sums[q], s)
+    return m, s
 
 
 def three_parts(x):
@@ -83,7 +79,7 @@
 
 def kernel(
     src_ref, fin_ref, growth_ref, live_ref, fates_ref, out_ref, pot_ref,
-    xst, fst, fates_st, xbuf, ybuf, xk, xt0, xt1, yt, yts, ct, cr, ub, vb, wt,
+    xst, fst, fates_st, xbuf, ybuf, xk, xt0, xt1, yt, yk, ysq, la, ct, cr, ub, vb, wt,
     csend, cslot, rsend, rslot, fsend, fother, hand, pbuf, pbf, chin, s1, s2st, s2,
     in_send, x_sem, y_sem, f_sem, fs_send, cs_send, cs_recv, rs_send, rs_recv,
     p_send, p_recv, ch_send, ch_recv, s1_send, s1_recv, s2_send, s2_recv,
@@ -166,15 +162,6 @@
 
     pl.semaphore_wait(barrier, expected)
 
-    for k, (cond, where) in enumerate(x_to):
-        @pl.when(cond)
-        def _(where=where):
-            push(xst, xbuf.at[z % 4], in_send, x_sem, at(*where)).start()
-
-    @pl.when(c == home)
-    def _():
-        pltpu.make_async_copy(xst, xbuf.at[z % 4], x_sem).start()
-
     for cond, where in y_to:
         @pl.when(cond)
         def _(where=where):
@@ -195,6 +182,15 @@
         def _(where=where):
             pltpu.make_async_copy(fst, fin_dst, y_sem).start()
             pltpu.make_async_copy(fates_st.at[where[2] // 2], fate_dst, f_sem).start()
+
+    for k, (cond, where) in enumerate(x_to):
+        @pl.when(cond)
+        def _(where=where):
+            push(xst, xbuf.at[z % 4], in_send, x_sem.at[z % 4], at(*where)).start()
+
+    @pl.when(c == home)
+    def _():
+        pltpu.make_async_copy(xst, xbuf.at[z % 4], x_sem.at[z % 4]).start()
 
     live_now = jnp.int32(0)
     live_next = jnp.int32(0)
@@ -209,150 +205,161 @@
     log_b = jnp.where(col_ids < live_next, -log_next, NEG)
 
     pltpu.make_async_copy(ybuf, ybuf, y_sem).wait()
-    keep = lax.broadcasted_iota(jnp.int32, (32, 512), 0) < 30
+    row_of = lax.broadcasted_iota(jnp.int32, (32, 512), 0)
+    keep = row_of < 30
     for k in range(2):
         cells = jnp.where(keep, ybuf[k], 0.0)
+        norms = jnp.sum(cells * cells, axis=0, keepdims=True)
+        for q in range(4):
+            flat = jnp.broadcast_to(norms[:, LANES * q : LANES * (q + 1)], (LANES, LANES))
+            first = 512 * k + LANES * q
+            vb[first : first + LANES, :] = jnp.transpose(flat)
         high, mid, low = three_parts(-2.0 * cells)
-        stack = jnp.concatenate([high, mid, low, high], axis=0)
+        stack = jnp.concatenate([jnp.where(row_of == 30, norms, high), mid, low, high], axis=0)
         yt[512 * k : 512 * (k + 1), :] = jnp.transpose(stack)
-
     for sub in range(8):
-        yts[LANES * sub : LANES * (sub + 1), :] = yt[pl.ds(sub, LANES, stride=8), :].astype(BF16)
-
-    def y_norms(k, packed):
-        for j in range(16):
-            row = pl.multiple_of((16 * k + j) * 8, 8)
-            tile = yt[pl.ds(row, 8), :]
-            whole = tile + pltpu.roll(tile, 96, axis=1) + pltpu.roll(tile, 64, axis=1)
-            whole = jnp.where(lanes < 32, whole, 0.0)
-            norm = jnp.broadcast_to(0.25 * jnp.sum(whole * whole, axis=1, keepdims=True), (8, LANES))
-            vb[pl.ds(row, 8), :] = norm
-            packed = jnp.where(lanes == 16 * k + j, norm, packed)
-        return packed
-
-    y_sq = lax.fori_loop(0, 8, y_norms, jnp.zeros((8, LANES), F32))
-
-    pltpu.make_async_copy(xbuf, xbuf, x_sem).wait()
-    x_rows = []
-    g_rows = []
-    for k in range(4):
-        cells = jnp.where(keep, xbuf[k], 0.0)
-        norms = jnp.sum(cells * cells, axis=0, keepdims=True)
-        x_rows += [norms[:, LANES * q : LANES * (q + 1)] for q in range(4)]
-        g_rows += [xbuf[k, 30:31, LANES * q : LANES * (q + 1)] for q in range(4)]
-        high, mid, low = three_parts(cells)
-        none = jnp.zeros_like(high)
-        for part, stack in enumerate(([high, high, high, none], [mid, mid, none, low])):
-            stack = jnp.concatenate(stack, axis=0)
-            xk[LANES * part : LANES * (part + 1), 512 * k : 512 * (k + 1)] = stack.astype(BF16)
-            turned = jnp.transpose(stack)
-            for q in range(4):
-                first = 1024 * (k // 2) + 4 * (k % 2) + q
-                (xt0, xt1)[part][pl.ds(first, LANES, stride=8), :] = turned[LANES * q : LANES * (q + 1), :]
-    x_sq = [jnp.concatenate(x_rows[8 * r : 8 * r + 8], axis=0) for r in range(2)]
-    grown = [jnp.concatenate(g_rows[8 * r : 8 * r + 8], axis=0) for r in range(2)]
-    log_a = [jnp.where(row_ids[r] < live_now, jnp.log2(grown[r]) - log_now, NEG) for r in range(2)]
+        turned = jnp.transpose(yt[pl.ds(sub, LANES, stride=8), :])
+        yk[:, LANES * sub : LANES * (sub + 1)] = turned.astype(BF16)
+        ysq[sub : sub + 1, :] = turned[30:31, :]
+
+    def merge(first, second):
+        peak = jnp.maximum(first[0], second[0])
+        return peak, first[1] * jnp.exp2(first[0] - peak) + second[1] * jnp.exp2(second[0] - peak)
+
+    columns = None
     for r in range(2):
-        spread_columns(x_sq[r], ub, 1024 * r)
-
-    def ct_rows(k, carry):
-        row = pl.multiple_of(k * 128, 128)
-        left = yt[pl.ds(row, 128), :].astype(BF16)
-        left = jnp.concatenate([left, left], axis=1)
-        cross = jnp.dot(left, xk[...], preferred_element_type=F32)
-        for q in range(16):
-            norm = vb[pl.ds(row, 128), :] + x_rows[q]
-            ct[pl.ds(row, 128), LANES * q : LANES * (q + 1)] = (
-                norm + cross[:, LANES * q : LANES * (q + 1)]
-            ) * COST_SCALE
-        return carry
-
-    lax.fori_loop(0, 8, ct_rows, 0)
-
-    def cr_rows(k, carry):
-        row = pl.multiple_of(k * 128, 128)
-        left = jnp.concatenate([xt0[pl.ds(row, 128), :], xt1[pl.ds(row, 128), :]], axis=1).astype(BF16)
-        right = yts[...]
-        right = jnp.concatenate([right, right], axis=1)
-        cross = lax.dot_general(left, right, (((1,), (1,)), ((), ())), preferred_element_type=F32)
-        for q in range(8):
-            norm = ub[pl.ds(row, 128), :] + y_sq[q : q + 1, :]
-            cr[pl.ds(row, 128), LANES * q : LANES * (q + 1)] = (
-                norm + cross[:, LANES * q : LANES * (q + 1)]
-            ) * COST_SCALE
-        return carry
-
-    lax.fori_loop(0, 16, cr_rows, 0)
-
-    for r in range(2):
-        spread_columns(log_a[r], ub, 1024 * r)
-
-    def iterate(step, carry):
-        par = step % 2
-        ((m0, s0),) = lse_pass(cr, ub, HALF, 8, 8)
+        x_rows = []
+        g_rows = []
+        for k in range(2 * r, 2 * r + 2):
+            block = xbuf.at[k]
+            pltpu.make_async_copy(block, block, x_sem.at[k]).wait()
+            cells = jnp.where(keep, xbuf[k], 0.0)
+            norms = jnp.sum(cells * cells, axis=0, keepdims=True)
+            x_rows += [norms[:, LANES * q : LANES * (q + 1)] for q in range(4)]
+            g_rows += [xbuf[k, 30:31, LANES * q : LANES * (q + 1)] for q in range(4)]
+            high, mid, low = three_parts(cells)
+            none = jnp.zeros_like(high)
+            for part, stack in enumerate(([high, high, high, none], [mid, mid, none, low])):
+                stack = jnp.concatenate(stack, axis=0)
+                xk[LANES * part : LANES * (part + 1), 512 * k : 512 * (k + 1)] = stack.astype(BF16)
+                turned = jnp.transpose(stack)
+                for q in range(4):
+                    first = 1024 * r + 4 * (k % 2) + q
+                    (xt0, xt1)[part][pl.ds(first, LANES, stride=8), :] = turned[LANES * q : LANES * (q + 1), :]
+        grown = jnp.concatenate(g_rows, axis=0)
+        log_a = jnp.where(row_ids[r] < live_now, jnp.log2(grown) - log_now, NEG)
+        la[r] = log_a
+        spread_columns(jnp.concatenate(x_rows, axis=0), ub, 1024 * r)
+
+        def ct_rows(k, carry, r=r, x_rows=x_rows):
+            row = pl.multiple_of(k * 256, 256)
+            left = yt[pl.ds(row, 256), :].astype(BF16)
+            left = jnp.concatenate([left, left], axis=1)
+            cross = jnp.dot(left, xk[:, 1024 * r : 1024 * (r + 1)], preferred_element_type=F32)
+            for q in range(8):
+                norm = vb[pl.ds(row, 256), :] + x_rows[q]
+                first = 1024 * r + LANES * q
+                ct[pl.ds(row, 256), first : first + LANES] = (
+                    norm + cross[:, LANES * q : LANES * (q + 1)]
+                ) * COST_SCALE
+            return carry
+
+        lax.fori_loop(0, 4, ct_rows, 0)
+
+        def cr_rows(k, carry, r=r):
+            row = pl.multiple_of(1024 * r + k * 256, 256)
+            left = jnp.concatenate([xt0[pl.ds(row, 256), :], xt1[pl.ds(row, 256), :]], axis=1).astype(BF16)
+            right = yk[...]
+            cross = jnp.dot(left, jnp.concatenate([right, right], axis=0), preferred_element_type=F32)
+            for q in range(8):
+                norm = ub[pl.ds(row, 256), :] + ysq[q : q + 1, :]
+                cr[pl.ds(row, 256), LANES * q : LANES * (q + 1)] = (
+                    norm + cross[:, LANES * q : LANES * (q + 1)]
+                ) * COST_SCALE
+            return carry
+
+        lax.fori_loop(0, 4, cr_rows, 0)
+        spread_columns(log_a, ub, 1024 * r)
+        found = lse_pass(cr, ub, 1024 * r, 0)
+        columns = found if columns is None else merge(columns, found)
+
+    def from_columns(par, m0, s0):
         csend[par, 0:8] = m0
         csend[par, 8:16] = s0
         copy = push(csend.at[par], cslot.at[par], cs_send.at[par], cs_recv.at[par], at(*core_peer))
         copy.start()
         copy.wait()
-        m1, s1_ = cslot[par, 0:8], cslot[par, 8:16]
-        peak = jnp.maximum(m0, m1)
-        total = s0 * jnp.exp2(m0 - peak) + s1_ * jnp.exp2(m1 - peak)
-        pot_v = -SHRINK * (peak + jnp.log2(total)) + log_b
-        spread_columns(pot_v, vb, 0)
-        rows = lse_pass(ct, vb, QUARTER, 16, 4)
-        for r in range(2):
-            rsend[par, 8 * r : 8 * r + 8] = rows[r][0]
-            rsend[par, 16 + 8 * r : 24 + 8 * r] = rows[r][1]
-        rslot[par, b] = rsend[par]
-        copies = [
-            push(rsend.at[par], rslot.at[par, b], rs_send.at[par], rs_recv.at[par], at(*where))
-            for where in row_peers
-        ]
-        for copy in copies:
-            copy.start()
-        three = rslot.at[par, pl.ds(0, 3)]
-        pltpu.make_async_copy(three, three, rs_recv.at[par]).wait()
-        out = []
-        for r in range(2):
-            ms = [rslot[par, k, 8 * r : 8 * r + 8] for k in range(4)]
-            ss = [rslot[par, k, 16 + 8 * r : 24 + 8 * r] for k in range(4)]
-            peak = jnp.maximum(jnp.maximum(ms[0], ms[1]), jnp.maximum(ms[2], ms[3]))
-            total = ss[0] * jnp.exp2(ms[0] - peak)
-            for k in range(1, 4):
-                total = total + ss[k] * jnp.exp2(ms[k] - peak)
-            level = -SHRINK * (peak + jnp.log2(total))
-            spread_columns(level + log_a[r], ub, 1024 * r)
-            out += [peak, total, level]
-        pltpu.make_async_copy(three, three, rs_send.at[par]).wait()
-        return tuple(out)
-
-    zero = jnp.zeros((8, LANES), F32)
-    final = lax.fori_loop(0, ITERS, iterate, (zero,) * 6)
+        peak, total = merge((m0, s0), (cslot[par, 0:8], cslot[par, 8:16]))
+        spread_columns(-SHRINK * (peak + jnp.log2(total)) + log_b, vb, 0)
+
+    def send_rows(par):
+        def half(r, carry):
+            m, s = lse_pass(ct, vb, 0, 1024 * r)
+            rsend[par, r, 0:8] = m
+            rsend[par, r, 8:16] = s
+            rslot[par, r, b, 0:8] = m
+            rslot[par, r, b, 8:16] = s
+            for where in row_peers:
+                push(
+                    rsend.at[par, r], rslot.at[par, r, b], rs_send.at[par, r], rs_recv.at[par, r], at(*where)
+                ).start()
+            return carry
+
+        lax.fori_loop(0, 2, half, 0)
+
+    def from_rows(par, r):
+        three = rslot.at[par, r, pl.ds(0, 3)]
+        pltpu.make_async_copy(three, three, rs_recv.at[par, r]).wait()
+        pltpu.make_async_copy(three, three, rs_send.at[par, r]).wait()
+        ms = [rslot[par, r, k, 0:8] for k in range(4)]
+        ss = [rslot[par, r, k, 8:16] for k in range(4)]
+        peak = jnp.maximum(jnp.maximum(ms[0], ms[1]), jnp.maximum(ms[2], ms[3]))
+        terms = [ss[k] * jnp.exp2(ms[k] - peak) for k in range(4)]
+        total = (terms[0] + terms[1]) + (terms[2] + terms[3])
+        return peak, total, -SHRINK * (peak + jnp.log2(total))
+
+    def iterate(step, carry):
+        par = step % 2
+        from_columns(par, *carry)
+        send_rows(par)
+
+        def half(r, so_far):
+            level = from_rows(par, r)[2]
+            spread_columns(level + la[r], ub, 1024 * r)
+            return merge(so_far, lse_pass(cr, ub, 1024 * r, 0))
+
+        return lax.fori_loop(0, 2, half, (jnp.full((8, LANES), LOWEST, F32), jnp.zeros((8, LANES), F32)))
+
+    columns = lax.fori_loop(0, ITERS - 1, iterate, columns)
+    par = (ITERS - 1) % 2
+    from_columns(par, *columns)
+    send_rows(par)
 
     for r in range(2):
-        fsend[8 * r : 8 * r + 8] = final[3 * r + 2] * (EPS / LOG2E)
+        wpeak = [rsend[par, r, q : q + 1, :] for q in range(8)]
+
+        def w_rows(k, carry, r=r, wpeak=wpeak):
+            for j in range(4):
+                row = pl.multiple_of(k * 64 + 16 * j, 16)
+                left = vb[pl.ds(row, 16), :]
+                for q in range(8):
+                    first = 1024 * r + LANES * q
+                    s = left - ct[pl.ds(row, 16), first : first + LANES]
+                    wt[pl.ds(row, 16), first : first + LANES] = jnp.exp2(s - wpeak[q]).astype(BF16)
+            return carry
+
+        lax.fori_loop(0, QUARTER // 64, w_rows, 0)
+
+    scales = []
+    for r in range(2):
+        peak, total, level = from_rows(par, r)
+        fsend[8 * r : 8 * r + 8] = level * (EPS / LOG2E)
+        scale = jnp.exp2(rsend[par, r, 0:8] - peak) / total
+        scale = jnp.where(row_ids[r] < live_now, scale, 0.0)
+        scales += [scale[q : q + 1, :] for q in range(8)]
+
     pot_copy = push(fsend, fother, p_send, p_recv, at(*core_peer))
     pot_copy.start()
-
-    wpeak = []
-    wscale = []
-    for r in range(2):
-        inv = 1.0 / final[3 * r + 1]
-        for q in range(8):
-            wpeak.append(final[3 * r][q : q + 1, :])
-            wscale.append(inv[q : q + 1, :])
-
-    def w_rows(k, carry):
-        row = pl.multiple_of(k * 16, 16)
-        left = vb[pl.ds(row, 16), :]
-        for q in range(16):
-            s = left - ct[pl.ds(row, 16), LANES * q : LANES * (q + 1)]
-            w = jnp.exp2(s - wpeak[q]) * wscale[q]
-            wt[pl.ds(row, 16), LANES * q : LANES * (q + 1)] = w.astype(BF16)
-        return carry
-
-    lax.fori_loop(0, QUARTER // 16, w_rows, 0)
 
     @pl.when(last)
     def _():
@@ -366,12 +373,12 @@
             total = total + chin[k].astype(F32)
         hand[...] = total.astype(BF16)
 
-    ids = HALF * c + lax.broadcasted_iota(jnp.int32, (16, HALF), 1)
-    part = jnp.dot(hand[...], wt[...], preferred_element_type=F32)
-    part = jnp.where(ids < live_now, part, 0.0)
-    pbuf[...] = part
-    pbf[0] = part[:, 0:QUARTER].astype(BF16)
-    pbf[1] = part[:, QUARTER:HALF].astype(BF16)
+    for r in range(2):
+        part = jnp.dot(hand[...], wt[:, 1024 * r : 1024 * (r + 1)], preferred_element_type=F32)
+        for q in range(8):
+            tile = part[:, LANES * q : LANES * (q + 1)] * scales[8 * r + q]
+            pbuf[:, 1024 * r + LANES * q : 1024 * r + LANES * (q + 1)] = tile
+            pbf[r, :, LANES * q : LANES * (q + 1)] = tile.astype(BF16)
     for k, (cond, where) in enumerate(ch_to):
         @pl.when(cond)
         def _(k=k, where=where):
@@ -452,14 +459,15 @@
         scratch_shapes=[
             V((32, 512), F32), V((32, 256), F32), V((4, 16, 256), BF16),
             V((4, 32, 512), F32), V((2, 32, 512), F32),
-            V((256, HALF), BF16), V((HALF, 128), F32), V((HALF, 128), F32), V((QUARTER, 128), F32), V((QUARTER, 128), BF16),
+            V((256, HALF), BF16), V((HALF, 128), F32), V((HALF, 128), F32), V((QUARTER, 128), F32), V((128, QUARTER), BF16),
+            V((8, 128), F32), V((2, 8, 128), F32),
             V((QUARTER, HALF), F32), V((HALF, QUARTER), F32),
             V((HALF, 128), F32), V((QUARTER, 128), F32), V((QUARTER, HALF), BF16),
-            V((2, 16, 128), F32), V((2, 16, 128), F32), V((2, 32, 128), F32), V((2, 4, 32, 128), F32),
+            V((2, 16, 128), F32), V((2, 16, 128), F32), V((2, 2, 16, 128), F32), V((2, 2, 4, 16, 128), F32),
             V((16, 128), F32), V((16, 128), F32),
             V((16, QUARTER), BF16), V((16, HALF), F32), V((2, 16, QUARTER), BF16), V((4, 16, QUARTER), BF16),
             V((4, 16, 128), F32), V((16, 128), F32), V((4, 16, 128), F32),
-            dma(()), dma(()), dma(()), dma(()), dma(()), dma((2,)), dma((2,)), dma((2,)), dma((2,)),
+            dma(()), dma((4,)), dma(()), dma(()), dma(()), dma((2,)), dma((2,)), dma((2, 2)), dma((2, 2)),
             dma(()), dma(()), dma(()), dma(()), dma(()), dma(()), dma(()), dma(()),
         ],
         compiler_params=pltpu.CompilerParams(

time: 156 us -> 151 us (0.968)
  Pallas kernels: 153 us -> 148 us
    pallas_call x1, Pallas kernels: 153 us -> 148 us  [local(): pl.pallas_call(kernel, out_shape=(jax.ShapeDtypeStruct((1, 40, 32), F32),...]
where the time goes in v2:
time: 151 us
  Pallas kernels  148 us (98%)
  local copies, waits for them, and re-layouts  2.14 us (1%)
    pallas_call x1, Pallas kernels, local(): pl.pallas_call(kernel, out_shape=(jax.ShapeDtypeStruct((1, 40, 32), F32),...  148 us

profile of v2, /device:TPU:1, one launch (start us, length us, event | category | flops | bytes accessed | tf_op | source)
XLA Modules:
  0.0 151.0 jit_solution(15726014686969751814)
XLA Ops:
  0.6 0.0 copy-start
  0.6 0.0 copy-start.3
  0.7 0.0 copy-start.2
  0.7 0.0 copy-start.1
  0.7 0.9 copy.7.src_ref
  1.5 0.0 copy-done
  1.5 0.0 copy-done.3
  1.5 0.0 copy-done.2
  1.6 0.0 copy-done.1
  1.6 148.2 %transport.1 = (f32[1,40,32]{2,1,0:T(8,128)S(1)}, f32[1,512]{1,0:T(1,128)S(1)}) custom-call(f32[1,30,512]{2,1,0:T(8,128)S(1)} %copy.7.src_ref, f32[30,256]{1,0:T(8,128)S(1)} %copy-done.1, f32[1,512]{1,0:T(1,128)S(1)} %copy-done.2, s32[5]{0:T(128)S(1)} %copy-done.3, f32[40,256]{1,0:T(8,128)S(1)} %copy-done), custom_call_target="tpu_custom_call" | custom-call | tf_op jit(solution)/shard_map/transport/pallas_call | solution.py:451
  149.8 0.7 copy.8
  150.4 0.6 copy.10
Async XLA Ops:
  0.6 0.9 copy-start
  0.6 0.9 copy-start.3
  0.7 0.9 copy-start.2
  0.7 0.9 copy-start.1

commit v3 on v2

--- a/solution.py
+++ b/solution.py
@@ -35,27 +35,28 @@
     return lax.broadcasted_iota(jnp.int32, (8, LANES), 0)
 
 
-def spread_columns(packed, dst, base):
+def spread_columns(packed, dst):
     for t in range(LANES):
-        row = pl.multiple_of(base + 8 * t, 8)
-        dst[pl.ds(row, 8), :] = jnp.broadcast_to(packed[:, t : t + 1], (8, LANES))
-
-
-def lse_pass(cost, spread, row0, lane0):
+        dst[8 * t : 8 * t + 8, :] = jnp.broadcast_to(packed[:, t : t + 1], (8, LANES))
+
+
+def lse_pass(cost, spread):
     tiles = 8
+    rows = 8 * GROUP
 
     def walk(start, update):
         def body(k, acc):
             acc = list(acc)
+            first = pl.multiple_of(k * rows, rows)
+            left_rows = spread.at[pl.ds(first, rows)]
+            cost_rows = cost.at[pl.ds(first, rows)]
             for t in range(GROUP):
-                row = pl.multiple_of(row0 + (k * GROUP + t) * 8, 8)
-                left = spread[pl.ds(row, 8), :]
+                left = left_rows[8 * t : 8 * t + 8, :]
                 for q in range(tiles):
-                    lane = pl.multiple_of(lane0 + LANES * q, LANES)
-                    acc[q] = update(q, acc[q], left - cost[pl.ds(row, 8), pl.ds(lane, LANES)])
+                    acc[q] = update(q, acc[q], left - cost_rows[8 * t : 8 * t + 8, LANES * q : LANES * (q + 1)])
             return tuple(acc)
 
-        return lax.fori_loop(0, QUARTER // (8 * GROUP), body, tuple(start))
+        return lax.fori_loop(0, QUARTER // rows, body, tuple(start))
 
     peaks = walk([jnp.full((8, LANES), LOWEST, F32)] * tiles, lambda q, a, s: jnp.maximum(a, s))
     peaks = [jnp.broadcast_to(jnp.max(a, axis=0, keepdims=True), (8, LANES)) for a in peaks]
@@ -249,7 +250,7 @@
         grown = jnp.concatenate(g_rows, axis=0)
         log_a = jnp.where(row_ids[r] < live_now, jnp.log2(grown) - log_now, NEG)
         la[r] = log_a
-        spread_columns(jnp.concatenate(x_rows, axis=0), ub, 1024 * r)
+        spread_columns(jnp.concatenate(x_rows, axis=0), ub.at[r])
 
         def ct_rows(k, carry, r=r, x_rows=x_rows):
             row = pl.multiple_of(k * 256, 256)
@@ -258,8 +259,7 @@
             cross = jnp.dot(left, xk[:, 1024 * r : 1024 * (r + 1)], preferred_element_type=F32)
             for q in range(8):
                 norm = vb[pl.ds(row, 256), :] + x_rows[q]
-                first = 1024 * r + LANES * q
-                ct[pl.ds(row, 256), first : first + LANES] = (
+                ct[r, pl.ds(row, 256), LANES * q : LANES * (q + 1)] = (
                     norm + cross[:, LANES * q : LANES * (q + 1)]
                 ) * COST_SCALE
             return carry
@@ -267,20 +267,21 @@
         lax.fori_loop(0, 4, ct_rows, 0)
 
         def cr_rows(k, carry, r=r):
-            row = pl.multiple_of(1024 * r + k * 256, 256)
-            left = jnp.concatenate([xt0[pl.ds(row, 256), :], xt1[pl.ds(row, 256), :]], axis=1).astype(BF16)
+            row = pl.multiple_of(k * 256, 256)
+            both = pl.multiple_of(1024 * r + k * 256, 256)
+            left = jnp.concatenate([xt0[pl.ds(both, 256), :], xt1[pl.ds(both, 256), :]], axis=1).astype(BF16)
             right = yk[...]
             cross = jnp.dot(left, jnp.concatenate([right, right], axis=0), preferred_element_type=F32)
             for q in range(8):
-                norm = ub[pl.ds(row, 256), :] + ysq[q : q + 1, :]
-                cr[pl.ds(row, 256), LANES * q : LANES * (q + 1)] = (
+                norm = ub[r, pl.ds(row, 256), :] + ysq[q : q + 1, :]
+                cr[r, pl.ds(row, 256), LANES * q : LANES * (q + 1)] = (
                     norm + cross[:, LANES * q : LANES * (q + 1)]
                 ) * COST_SCALE
             return carry
 
         lax.fori_loop(0, 4, cr_rows, 0)
-        spread_columns(log_a, ub, 1024 * r)
-        found = lse_pass(cr, ub, 1024 * r, 0)
+        spread_columns(log_a, ub.at[r])
+        found = lse_pass(cr.at[r], ub.at[r])
         columns = found if columns is None else merge(columns, found)
 
     def from_columns(par, m0, s0):
@@ -290,11 +291,11 @@
         copy.start()
         copy.wait()
         peak, total = merge((m0, s0), (cslot[par, 0:8], cslot[par, 8:16]))
-        spread_columns(-SHRINK * (peak + jnp.log2(total)) + log_b, vb, 0)
+        spread_columns(-SHRINK * (peak + jnp.log2(total)) + log_b, vb)
 
     def send_rows(par):
         def half(r, carry):
-            m, s = lse_pass(ct, vb, 0, 1024 * r)
+            m, s = lse_pass(ct.at[r], vb)
             rsend[par, r, 0:8] = m
             rsend[par, r, 8:16] = s
             rslot[par, r, b, 0:8] = m
@@ -325,8 +326,8 @@
 
         def half(r, so_far):
             level = from_rows(par, r)[2]
-            spread_columns(level + la[r], ub, 1024 * r)
-            return merge(so_far, lse_pass(cr, ub, 1024 * r, 0))
+            spread_columns(level + la[r], ub.at[r])
+            return merge(so_far, lse_pass(cr.at[r], ub.at[r]))
 
         return lax.fori_loop(0, 2, half, (jnp.full((8, LANES), LOWEST, F32), jnp.zeros((8, LANES), F32)))
 
@@ -344,7 +345,7 @@
                 left = vb[pl.ds(row, 16), :]
                 for q in range(8):
                     first = 1024 * r + LANES * q
-                    s = left - ct[pl.ds(row, 16), first : first + LANES]
+                    s = left - ct[r, pl.ds(row, 16), LANES * q : LANES * (q + 1)]
                     wt[pl.ds(row, 16), first : first + LANES] = jnp.exp2(s - wpeak[q]).astype(BF16)
             return carry
 
@@ -461,8 +462,8 @@
             V((4, 32, 512), F32), V((2, 32, 512), F32),
             V((256, HALF), BF16), V((HALF, 128), F32), V((HALF, 128), F32), V((QUARTER, 128), F32), V((128, QUARTER), BF16),
             V((8, 128), F32), V((2, 8, 128), F32),
-            V((QUARTER, HALF), F32), V((HALF, QUARTER), F32),
-            V((HALF, 128), F32), V((QUARTER, 128), F32), V((QUARTER, HALF), BF16),
+            V((2, QUARTER, QUARTER), F32), V((2, QUARTER, QUARTER), F32),
+            V((2, QUARTER, 128), F32), V((QUARTER, 128), F32), V((QUARTER, HALF), BF16),
             V((2, 16, 128), F32), V((2, 16, 128), F32), V((2, 2, 16, 128), F32), V((2, 2, 4, 16, 128), F32),
             V((16, 128), F32), V((16, 128), F32),
             V((16, QUARTER), BF16), V((16, HALF), F32), V((2, 16, QUARTER), BF16), V((4, 16, QUARTER), BF16),

time: 151 us -> 123 us (0.81)
  Pallas kernels: 148 us -> 120 us
    pallas_call x1, Pallas kernels: 148 us -> 120 us  [local(): pl.pallas_call(kernel, out_shape=(jax.ShapeDtypeStruct((1, 40, 32), F32),...]
where the time goes in v3:
time: 123 us
  Pallas kernels  120 us (98%)
  local copies, waits for them, and re-layouts  2.14 us (2%)
    pallas_call x1, Pallas kernels, local(): pl.pallas_call(kernel, out_shape=(jax.ShapeDtypeStruct((1, 40, 32), F32),...  120 us

profile of v3, /device:TPU:1, one launch (start us, length us, event | category | flops | bytes accessed | tf_op | source)
XLA Modules:
  0.0 122.9 jit_solution(130840515274393344)
XLA Ops:
  0.6 0.0 copy-start
  0.6 0.0 copy-start.3
  0.7 0.0 copy-start.2
  0.7 0.0 copy-start.1
  0.7 0.9 copy.7.src_ref
  1.5 0.0 copy-done
  1.5 0.0 copy-done.3
  1.5 0.0 copy-done.2
  1.6 0.0 copy-done.1
  1.6 120.1 %transport.1 = (f32[1,40,32]{2,1,0:T(8,128)S(1)}, f32[1,512]{1,0:T(1,128)S(1)}) custom-call(f32[1,30,512]{2,1,0:T(8,128)S(1)} %copy.7.src_ref, f32[30,256]{1,0:T(8,128)S(1)} %copy-done.1, f32[1,512]{1,0:T(1,128)S(1)} %copy-done.2, s32[5]{0:T(128)S(1)} %copy-done.3, f32[40,256]{1,0:T(8,128)S(1)} %copy-done), custom_call_target="tpu_custom_call" | custom-call | tf_op jit(solution)/shard_map/transport/pallas_call | solution.py:452
  121.7 0.7 copy.8
  122.3 0.6 copy.10
Async XLA Ops:
  0.6 0.9 copy-start
  0.6 0.9 copy-start.3
  0.7 0.9 copy-start.2
  0.7 0.9 copy-start.1

commit v4 on v3

--- a/solution.py
+++ b/solution.py
@@ -81,9 +81,9 @@
 def kernel(
     src_ref, fin_ref, growth_ref, live_ref, fates_ref, out_ref, pot_ref,
     xst, fst, fates_st, xbuf, ybuf, xk, xt0, xt1, yt, yk, ysq, la, ct, cr, ub, vb, wt,
-    csend, cslot, rsend, rslot, fsend, fother, hand, pbuf, pbf, chin, s1, s2st, s2,
+    csend, cslot, rsend, rslot, fsend, fother, hand, pbuf, pbf, chin, s2,
     in_send, x_sem, y_sem, f_sem, fs_send, cs_send, cs_recv, rs_send, rs_recv,
-    p_send, p_recv, ch_send, ch_recv, s1_send, s1_recv, s2_send, s2_recv,
+    p_send, p_recv, ch_send, ch_recv, yf_send, yf_recv, s2_send, s2_recv, hx_send, hx_recv,
 ):
     p = lax.axis_index("pair")
     z = lax.axis_index("src")
@@ -120,11 +120,13 @@
     f_from = [(p, z, 2 * b + k // 2, k % 2) for k in range(4)]
     ch_to = [(p > 0, (down, *chip_at(2 * c + k // 2), k % 2)) for k in range(4)]
     ch_from = [(p < 3, (up, *chip_at(k), b // 2)) for k in range(4)]
-    s1_to = [(p, z0 + k // 4, y0 + (k % 4) // 2, k % 2) for k in range(8)]
-    s1_from = [(p, *chip_at(k), home) for k in range(4)]
     quad = 2 * yb + c
-    s2_to = [(p, z, 2 * quad + k // 2, k % 2) for k in range(4)]
-    s2_from = [(p, z, 2 * k + d // 2, d % 2) for k in range(4)]
+
+    def out_to(k):
+        return p, z0 + k // 16, 2 * (k // 4 % 4) + k // 2 % 2, k % 2
+
+    def out_from(k):
+        return p, z0 + k // 8, 2 * (k // 2 % 4) + k % 2, home
 
     barrier = pltpu.get_barrier_semaphore()
     expected = jnp.int32(4)
@@ -141,19 +143,16 @@
         greet(cond, where)
     for where in f_from:
         greet(last & jnp.logical_not(same(*where)), where)
-    for where in s1_from + s2_from:
-        greet(jnp.logical_not(same(*where)), where)
+    for k in range(16):
+        greet(jnp.logical_not(same(*out_from(k))), out_from(k))
     for cond, where in x_to + y_to + ch_to:
         expected = expected + jnp.where(cond, 1, 0)
     for where in f_to:
         expected = expected + jnp.where(f_active & jnp.logical_not(same(*where)), 1, 0)
-    for where in s1_to:
-        expected = expected + jnp.where((c == home) & jnp.logical_not(same(*where)), 1, 0)
-    for where in s2_to:
-        expected = expected + jnp.where(jnp.logical_not(same(*where)), 1, 0)
+    expected = expected + jnp.where(c == home, 31, 0)
 
     xst[30:32, :] = jnp.zeros((2, 512), F32)
-    xst[0:30, :] = src_ref[0]
+    xst[0:30, :] = src_ref[:, 0, :]
     xst[30:31, :] = growth_ref[...]
     fst[...] = jnp.zeros_like(fst)
     fst[0:30, :] = fin_ref[...]
@@ -163,20 +162,27 @@
 
     pl.semaphore_wait(barrier, expected)
 
+    def my_lanes(ref):
+        first = pl.multiple_of(256 * c, 256)
+        return ref.at[:, pl.ds(first, 256)]
+
     for cond, where in y_to:
         @pl.when(cond)
         def _(where=where):
-            push(xst, ybuf.at[zb], in_send, y_sem, at(*where)).start()
+            push(my_lanes(xst), my_lanes(ybuf.at[zb]), in_send, y_sem, at(*where)).start()
 
     slot = t % 4
     fin_dst = ybuf.at[slot // 2, :, pl.ds(pl.multiple_of((slot % 2) * 256, 256), 256)]
-    fate_dst = hand.at[:, pl.ds(pl.multiple_of(slot * 256, 256), 256)]
+    fate_dst = hand.at[slot // 2, :, pl.ds(pl.multiple_of((slot % 2) * 256, 256), 256)]
     for where in f_to:
         mine = same(*where)
 
+        @pl.when(f_active & jnp.logical_not(mine) & (where[3] == c))
+        def _(where=where):
+            push(fst, fin_dst, fs_send, y_sem, at(*where)).start()
+
         @pl.when(f_active & jnp.logical_not(mine))
         def _(where=where):
-            push(fst, fin_dst, fs_send, y_sem, at(*where)).start()
             push(fates_st.at[where[2] // 2], fate_dst, fs_send, f_sem, at(*where)).start()
 
         @pl.when(f_active & mine)
@@ -184,14 +190,17 @@
             pltpu.make_async_copy(fst, fin_dst, y_sem).start()
             pltpu.make_async_copy(fates_st.at[where[2] // 2], fate_dst, f_sem).start()
 
-    for k, (cond, where) in enumerate(x_to):
-        @pl.when(cond)
-        def _(where=where):
-            push(xst, xbuf.at[z % 4], in_send, x_sem.at[z % 4], at(*where)).start()
-
-    @pl.when(c == home)
-    def _():
-        pltpu.make_async_copy(xst, xbuf.at[z % 4], x_sem.at[z % 4]).start()
+    def send_cells(chosen):
+        for cond, where in x_to:
+            @pl.when(cond & chosen)
+            def _(where=where):
+                push(xst, xbuf.at[z % 4], in_send, x_sem.at[z % 4], at(*where)).start()
+
+        @pl.when((c == home) & chosen)
+        def _():
+            pltpu.make_async_copy(xst, xbuf.at[z % 4], x_sem.at[z % 4]).start()
+
+    send_cells(z % 4 < 2)
 
     live_now = jnp.int32(0)
     live_next = jnp.int32(0)
@@ -205,7 +214,13 @@
     col_ids = QUARTER * b + 8 * lanes + subs
     log_b = jnp.where(col_ids < live_next, -log_next, NEG)
 
-    pltpu.make_async_copy(ybuf, ybuf, y_sem).wait()
+    half = ybuf.at[:, :, pl.ds(0, 256)]
+    pltpu.make_async_copy(half, half, y_sem).wait()
+    mine = ybuf.at[:, :, pl.ds(pl.multiple_of(256 * c, 256), 256)]
+    y_copy = push(mine, mine, yf_send, yf_recv, at(*core_peer))
+    y_copy.start()
+    send_cells(z % 4 >= 2)
+    y_copy.wait()
     row_of = lax.broadcasted_iota(jnp.int32, (32, 512), 0)
     keep = row_of < 30
     for k in range(2):
@@ -344,20 +359,30 @@
                 row = pl.multiple_of(k * 64 + 16 * j, 16)
                 left = vb[pl.ds(row, 16), :]
                 for q in range(8):
-                    first = 1024 * r + LANES * q
                     s = left - ct[r, pl.ds(row, 16), LANES * q : LANES * (q + 1)]
-                    wt[pl.ds(row, 16), first : first + LANES] = jnp.exp2(s - wpeak[q]).astype(BF16)
+                    cr[r, pl.ds(row, 16), LANES * q : LANES * (q + 1)] = jnp.exp2(s - wpeak[q])
             return carry
 
         lax.fori_loop(0, QUARTER // 64, w_rows, 0)
 
-    scales = []
     for r in range(2):
         peak, total, level = from_rows(par, r)
         fsend[8 * r : 8 * r + 8] = level * (EPS / LOG2E)
         scale = jnp.exp2(rsend[par, r, 0:8] - peak) / total
         scale = jnp.where(row_ids[r] < live_now, scale, 0.0)
-        scales += [scale[q : q + 1, :] for q in range(8)]
+        scales = [scale[q : q + 1, :] for q in range(8)]
+
+        def round_rows(k, carry, r=r, scales=scales):
+            for j in range(4):
+                row = pl.multiple_of(k * 64 + 16 * j, 16)
+                for q in range(8):
+                    first = 1024 * r + LANES * q
+                    w = cr[r, pl.ds(row, 16), LANES * q : LANES * (q + 1)] * scales[q]
+                    wt[pl.ds(row, 16), first : first + LANES] = w.astype(BF16)
+            return carry
+
+        lax.fori_loop(0, QUARTER // 64, round_rows, 0)
+
 
     pot_copy = push(fsend, fother, p_send, p_recv, at(*core_peer))
     pot_copy.start()
@@ -369,49 +394,51 @@
     @pl.when(jnp.logical_not(last))
     def _():
         pltpu.make_async_copy(chin, chin, ch_recv).wait()
-        total = chin[0].astype(F32)
-        for k in range(1, 4):
-            total = total + chin[k].astype(F32)
-        hand[...] = total.astype(BF16)
-
+        total = (chin[0] + chin[1]) + (chin[2] + chin[3])
+        none = jnp.zeros((6, LANES), F32)
+        for q in range(4):
+            most = total[:, LANES * q : LANES * (q + 1)]
+            tile = jnp.concatenate([most, total[2 * q : 2 * q + 2, 512:640], none], axis=0)
+            hand[c, :, LANES * q : LANES * (q + 1)] = tile.astype(BF16)
+        copy = push(hand.at[c], hand.at[c], hx_send, hx_recv, at(*core_peer))
+        copy.start()
+        copy.wait()
+
+    handed = jnp.concatenate([hand[0], hand[1]], axis=1)
     for r in range(2):
-        part = jnp.dot(hand[...], wt[:, 1024 * r : 1024 * (r + 1)], preferred_element_type=F32)
+        tiles = []
+        part = jnp.dot(handed, wt[:, 1024 * r : 1024 * (r + 1)], preferred_element_type=F32)
         for q in range(8):
-            tile = part[:, LANES * q : LANES * (q + 1)] * scales[8 * r + q]
-            pbuf[:, 1024 * r + LANES * q : 1024 * r + LANES * (q + 1)] = tile
-            pbf[r, :, LANES * q : LANES * (q + 1)] = tile.astype(BF16)
+            tile = part[:, LANES * q : LANES * (q + 1)]
+            pbuf[8 * r + q] = tile
+            tiles.append(tile)
+        for h in range(2):
+            for q in range(4):
+                pbf[r, h, :, LANES * q : LANES * (q + 1)] = tiles[4 * h + q][0:8]
+            pbf[r, h, :, 512:640] = jnp.concatenate([tiles[4 * h + q][8:10] for q in range(4)], axis=0)
     for k, (cond, where) in enumerate(ch_to):
         @pl.when(cond)
         def _(k=k, where=where):
-            push(pbf.at[k // 2], chin.at[b], ch_send, ch_recv, at(*where)).start()
-
-    def s1_src(k):
-        first = pl.multiple_of(QUARTER * (a % 2) + LANES * k, LANES)
-        return pbuf.at[:, pl.ds(first, LANES)]
-
-    for k, where in enumerate(s1_to):
-        mine = same(*where)
-
-        @pl.when((c == home) & jnp.logical_not(mine))
-        def _(k=k, where=where):
-            push(s1_src(k), s1.at[b], s1_send, s1_recv, at(*where)).start()
-
-        @pl.when((c == home) & mine)
-        def _(k=k):
-            pltpu.make_async_copy(s1_src(k), s1.at[b], s1_recv).start()
-
-    pltpu.make_async_copy(s1, s1, s1_recv).wait()
-    s2st[...] = (s1[0] + s1[1]) + (s1[2] + s1[3])
-    for where in s2_to:
-        mine = same(*where)
-
-        @pl.when(jnp.logical_not(mine))
-        def _(where=where):
-            push(s2st, s2.at[d], s2_send, s2_recv, at(*where)).start()
-
-        @pl.when(mine)
-        def _():
-            pltpu.make_async_copy(s2st, s2.at[d], s2_recv).start()
+            push(pbf.at[k // 2, k % 2], chin.at[b], ch_send, ch_recv, at(*where)).start()
+
+    @pl.when(c == home)
+    def _():
+        def send_out(k, carry):
+            where = out_to(k)
+            tile = pbuf.at[8 * (a % 2) + k // 4]
+            mine = same(*where)
+
+            @pl.when(jnp.logical_not(mine))
+            def _():
+                push(tile, s2.at[d, b], s2_send, s2_recv, at(*where)).start()
+
+            @pl.when(mine)
+            def _():
+                pltpu.make_async_copy(tile, s2.at[d, b], s2_recv).start()
+
+            return carry
+
+        lax.fori_loop(0, 32, send_out, 0)
 
     pot_copy.wait()
     own = jnp.where(c == home, fsend[...], fother[...])
@@ -424,25 +451,27 @@
     pltpu.make_async_copy(s2, s2, s2_recv).wait()
     turn = lax.rem(LANES - 32 * quad, LANES)
     for g in range(4):
-        out_ref[0, 10 * g : 10 * g + 10, :] = pltpu.roll(s2[g], turn, axis=1)[0:10, 0:32]
+        four = [s2[g, k] for k in range(4)]
+        tile = (four[0] + four[1]) + (four[2] + four[3])
+        out_ref[0, 10 * g : 10 * g + 10, :] = pltpu.roll(tile, turn, axis=1)[0:10, 0:32]
 
     def settle(cond, ref, sem):
         @pl.when(cond)
         def _():
             pltpu.make_async_copy(ref, ref, sem).wait()
 
-    for cond, where in x_to + y_to:
+    for cond, where in x_to:
         settle(cond, xst, in_send)
+    for cond, where in y_to:
+        settle(cond, fst, in_send)
     for where in f_to:
         off = f_active & jnp.logical_not(same(*where))
-        settle(off, fst, fs_send)
+        settle(off & (where[3] == c), fst, fs_send)
         settle(off, fates_st.at[0], fs_send)
     for cond, where in ch_to:
-        settle(cond, pbf.at[0], ch_send)
-    for where in s1_to:
-        settle((c == home) & jnp.logical_not(same(*where)), s2st, s1_send)
-    for where in s2_to:
-        settle(jnp.logical_not(same(*where)), s2st, s2_send)
+        settle(cond, pbf.at[0, 0], ch_send)
+    settle(c == home, pbuf, s2_send)
+    settle(c == home, pbuf.at[pl.ds(0, 15)], s2_send)
 
 
 def local(src_cells, final_cells, growth, live, final_fates):
@@ -466,16 +495,16 @@
             V((2, QUARTER, 128), F32), V((QUARTER, 128), F32), V((QUARTER, HALF), BF16),
             V((2, 16, 128), F32), V((2, 16, 128), F32), V((2, 2, 16, 128), F32), V((2, 2, 4, 16, 128), F32),
             V((16, 128), F32), V((16, 128), F32),
-            V((16, QUARTER), BF16), V((16, HALF), F32), V((2, 16, QUARTER), BF16), V((4, 16, QUARTER), BF16),
-            V((4, 16, 128), F32), V((16, 128), F32), V((4, 16, 128), F32),
+            V((2, 16, 512), BF16), V((16, 16, 128), F32), V((2, 2, 8, 640), F32), V((4, 8, 640), F32),
+            V((4, 4, 16, 128), F32),
             dma(()), dma((4,)), dma(()), dma(()), dma(()), dma((2,)), dma((2,)), dma((2, 2)), dma((2, 2)),
-            dma(()), dma(()), dma(()), dma(()), dma(()), dma(()), dma(()), dma(()),
+            dma(()), dma(()), dma(()), dma(()), dma(()), dma(()), dma(()), dma(()), dma(()), dma(()),
         ],
         compiler_params=pltpu.CompilerParams(
             collective_id=0, has_side_effects=True, vmem_limit_bytes=48 * 2**20
         ),
         name="transport",
-    )(src_cells, final_cells, growth, live, final_fates))
+    )(jnp.transpose(src_cells, (1, 0, 2)), final_cells, growth, live, final_fates))
 
 
 def solution(mesh):

time: 123 us -> 122 us (level)
  Pallas kernels: 120 us -> 116 us
  local copies, waits for them, and re-layouts: 2.14 us -> 4.95 us
    pallas_call x1, Pallas kernels: 120 us -> 116 us  [local(): pl.pallas_call(kernel, out_shape=(jax.ShapeDtypeStruct((1, 40, 32), F32),...]
    unnamed x10 -> x11, local copies, waits for them, and re-layouts: 1.46 us -> 4.27 us
where the time goes in v4:
time: 122 us; the launch traced here: 121 us
  Pallas kernels  116 us (95%)
  local copies, waits for them, and re-layouts  4.95 us (4%)
    pallas_call x1, Pallas kernels, local(): pl.pallas_call(kernel, out_shape=(jax.ShapeDtypeStruct((1, 40, 32), F32),...  116 us
    unnamed x11, local copies, waits for them, and re-layouts  4.27 us

profile of v4, /device:TPU:1, one launch (start us, length us, event | category | flops | bytes accessed | tf_op | source)
XLA Modules:
  0.0 121.4 jit_solution(4726140233177947589)
XLA Ops:
  0.6 0.0 copy-start.4
  0.6 0.6 copy-done.4
  1.3 0.0 copy-start
  1.3 0.8 copy-done
  2.1 0.0 copy-start.1
  2.1 0.8 copy-done.1
  2.9 0.0 copy-start.2
  2.9 0.8 copy-done.2
  3.7 0.0 copy-start.3
  3.7 0.7 copy-done.3
  4.3 115.8 %transport.1 = (f32[1,40,32]{2,1,0:T(8,128)S(1)}, f32[1,512]{1,0:T(1,128)S(1)}) custom-call(f32[30,1,512]{2,1,0:T(1,128)S(1)} %bitcast.1, f32[30,256]{1,0:T(8,128)S(1)} %copy-done.2, f32[1,512]{1,0:T(1,128)S(1)} %copy-done.3, s32[5]{0:T(128)S(1)} %copy-done.4, f32[40,256]{1,0:T(8,128)S(1)} %copy-done.1), custom_call_target="tpu_custom_call" | custom-call | tf_op jit(solution)/shard_map/transport/pallas_call | solution.py:481
  120.1 0.7 copy.7
  120.8 0.6 copy.9
Async XLA Ops:
  0.6 0.7 copy-start.4
  1.3 0.8 copy-start
  2.1 0.8 copy-start.1
  2.9 0.8 copy-start.2
  3.7 0.7 copy-start.3

commit v5 on v4

--- a/solution.py
+++ b/solution.py
@@ -24,7 +24,7 @@
 HALF = 2048
 QUARTER = 1024
 LANES = 128
-GROUP = 32
+GROUP = 64
 
 
 def lane_iota():
@@ -106,11 +106,11 @@
         return (pp == p) & (zz == z) & (yy == y) & (cc == c)
 
     up, down = jnp.minimum(p + 1, 3), jnp.maximum(p - 1, 0)
-    chips = [((b + k) % 4) for k in range(1, 4)]
+    chips = [3 - b, (b + 2) % 4, b + 1 - 2 * (b % 2)]
     chip_at = lambda bb: (z0 + bb // 2, y0 + bb % 2)
     core_peer = (p, z, y, 1 - c)
     row_peers = [(p, *chip_at(bb), c) for bb in chips]
-    x_to = [(c == home, (p, (z + k) % 8, y, c)) for k in range(1, 8)]
+    x_to = [(c == home, (p, (z + k) % 8, y, c)) for k in (4, 3, 5, 2, 6, 1, 7)]
     x_from = [(4 * c + k != z, (p, 4 * c + k, y, c)) for k in range(4)]
     y_active = (p > 0) & (yb == a % 2)
     y_to = [(y_active, (down, home + 2 * k, y, c)) for k in range(4)]
@@ -410,7 +410,7 @@
         part = jnp.dot(handed, wt[:, 1024 * r : 1024 * (r + 1)], preferred_element_type=F32)
         for q in range(8):
             tile = part[:, LANES * q : LANES * (q + 1)]
-            pbuf[8 * r + q] = tile
+            pbuf[8 * r + q] = tile.astype(BF16)
             tiles.append(tile)
         for h in range(2):
             for q in range(4):
@@ -451,7 +451,7 @@
     pltpu.make_async_copy(s2, s2, s2_recv).wait()
     turn = lax.rem(LANES - 32 * quad, LANES)
     for g in range(4):
-        four = [s2[g, k] for k in range(4)]
+        four = [s2[g, k].astype(F32) for k in range(4)]
         tile = (four[0] + four[1]) + (four[2] + four[3])
         out_ref[0, 10 * g : 10 * g + 10, :] = pltpu.roll(tile, turn, axis=1)[0:10, 0:32]
 
@@ -495,8 +495,8 @@
             V((2, QUARTER, 128), F32), V((QUARTER, 128), F32), V((QUARTER, HALF), BF16),
             V((2, 16, 128), F32), V((2, 16, 128), F32), V((2, 2, 16, 128), F32), V((2, 2, 4, 16, 128), F32),
             V((16, 128), F32), V((16, 128), F32),
-            V((2, 16, 512), BF16), V((16, 16, 128), F32), V((2, 2, 8, 640), F32), V((4, 8, 640), F32),
-            V((4, 4, 16, 128), F32),
+            V((2, 16, 512), BF16), V((16, 16, 128), BF16), V((2, 2, 8, 640), F32), V((4, 8, 640), F32),
+            V((4, 4, 16, 128), BF16),
             dma(()), dma((4,)), dma(()), dma(()), dma(()), dma((2,)), dma((2,)), dma((2, 2)), dma((2, 2)),
             dma(()), dma(()), dma(()), dma(()), dma(()), dma(()), dma(()), dma(()), dma(()), dma(()),
         ],

time: 122 us -> 119 us (0.975)
  Pallas kernels: 116 us -> 113 us
    pallas_call x1, Pallas kernels: 116 us -> 113 us  [local(): pl.pallas_call(kernel, out_shape=(jax.ShapeDtypeStruct((1, 40, 32), F32),...]
where the time goes in v5:
time: 119 us
  Pallas kernels  113 us (95%)
  local copies, waits for them, and re-layouts  4.95 us (4%)
    pallas_call x1, Pallas kernels, local(): pl.pallas_call(kernel, out_shape=(jax.ShapeDtypeStruct((1, 40, 32), F32),...  113 us
    unnamed x11, local copies, waits for them, and re-layouts  4.27 us

profile of v5, /device:TPU:1, one launch (start us, length us, event | category | flops | bytes accessed | tf_op | source)
XLA Modules:
  0.0 118.8 jit_solution(11383560025918476156)
XLA Ops:
  0.6 0.0 copy-start.4
  0.6 0.6 copy-done.4
  1.3 0.0 copy-start
  1.3 0.8 copy-done
  2.1 0.0 copy-start.1
  2.1 0.8 copy-done.1
  2.9 0.0 copy-start.2
  2.9 0.8 copy-done.2
  3.7 0.0 copy-start.3
  3.7 0.7 copy-done.3
  4.3 113.2 %transport.1 = (f32[1,40,32]{2,1,0:T(8,128)S(1)}, f32[1,512]{1,0:T(1,128)S(1)}) custom-call(f32[30,1,512]{2,1,0:T(1,128)S(1)} %bitcast.1, f32[30,256]{1,0:T(8,128)S(1)} %copy-done.2, f32[1,512]{1,0:T(1,128)S(1)} %copy-done.3, s32[5]{0:T(128)S(1)} %copy-done.4, f32[40,256]{1,0:T(8,128)S(1)} %copy-done.1), custom_call_target="tpu_custom_call" | custom-call | tf_op jit(solution)/shard_map/transport/pallas_call | solution.py:481
  117.5 0.7 copy.7
  118.2 0.6 copy.9
Async XLA Ops:
  0.6 0.7 copy-start.4
  1.3 0.8 copy-start
  2.1 0.8 copy-start.1
  2.9 0.8 copy-start.2
  3.7 0.7 copy-start.3

commit v6 on v5

--- a/solution.py
+++ b/solution.py
@@ -416,10 +416,11 @@
             for q in range(4):
                 pbf[r, h, :, LANES * q : LANES * (q + 1)] = tiles[4 * h + q][0:8]
             pbf[r, h, :, 512:640] = jnp.concatenate([tiles[4 * h + q][8:10] for q in range(4)], axis=0)
-    for k, (cond, where) in enumerate(ch_to):
-        @pl.when(cond)
-        def _(k=k, where=where):
-            push(pbf.at[k // 2, k % 2], chin.at[b], ch_send, ch_recv, at(*where)).start()
+            cond, where = ch_to[2 * r + h]
+
+            @pl.when(cond)
+            def _(r=r, h=h, where=where):
+                push(pbf.at[r, h], chin.at[b], ch_send, ch_recv, at(*where)).start()
 
     @pl.when(c == home)
     def _():

time: 119 us -> 119 us (level)
  no operation moved by 1% of the time
where the time goes in v6:
time: 119 us
  Pallas kernels  113 us (95%)
  local copies, waits for them, and re-layouts  4.95 us (4%)
    pallas_call x1, Pallas kernels, local(): pl.pallas_call(kernel, out_shape=(jax.ShapeDtypeStruct((1, 40, 32), F32),...  113 us
    unnamed x11, local copies, waits for them, and re-layouts  4.27 us

profile of v6, /device:TPU:1, one launch (start us, length us, event | category | flops | bytes accessed | tf_op | source)
XLA Modules:
  0.0 118.6 jit_solution(7314481316529544983)
XLA Ops:
  0.6 0.0 copy-start.4
  0.6 0.6 copy-done.4
  1.3 0.0 copy-start
  1.3 0.8 copy-done
  2.1 0.0 copy-start.1
  2.1 0.8 copy-done.1
  2.9 0.0 copy-start.2
  2.9 0.8 copy-done.2
  3.7 0.0 copy-start.3
  3.7 0.7 copy-done.3
  4.3 113.0 %transport.1 = (f32[1,40,32]{2,1,0:T(8,128)S(1)}, f32[1,512]{1,0:T(1,128)S(1)}) custom-call(f32[30,1,512]{2,1,0:T(1,128)S(1)} %bitcast.1, f32[30,256]{1,0:T(8,128)S(1)} %copy-done.2, f32[1,512]{1,0:T(1,128)S(1)} %copy-done.3, s32[5]{0:T(128)S(1)} %copy-done.4, f32[40,256]{1,0:T(8,128)S(1)} %copy-done.1), custom_call_target="tpu_custom_call" | custom-call | tf_op jit(solution)/shard_map/transport/pallas_call | solution.py:482
  117.3 0.7 copy.7
  118.0 0.6 copy.9
Async XLA Ops:
  0.6 0.7 copy-start.4
  1.3 0.8 copy-start
  2.1 0.8 copy-start.1
  2.9 0.8 copy-start.2
  3.7 0.7 copy-start.3
